TPU v7x, 32 devices: a whole 2x2x4 slice. The times are simulated.
32 devices in a mesh: rep: 8 (over z, y), shard: 4 (over x, core).
Axes of the slice: x: 2, y: 2, z: 4, core: 2. Of those that a mesh axis runs over, the one named last changes fastest.
Arguments:
- tokens: bfloat16 [2, 16384, 1280], P(None, ('rep', 'shard')), may hold values from -6 to 6
- cotangent: bfloat16 [2, 16384, 1280], P(None, ('rep', 'shard')), may hold values from -6 to 6
- block_map: int32 [2, 8, 4], P(None, 'rep'), may hold values from 0 to 3, each once within a row
- query_weight: bfloat16 [1280, 1280], P('shard'), may hold values from -0.15625 to 0.15625
- key_weight: bfloat16 [1280, 320], P('shard'), may hold values from -0.15625 to 0.15625
- value_weight: bfloat16 [1280, 320], P('shard'), may hold values from -0.15625 to 0.15625
- output_weight: bfloat16 [1280, 1280], P('shard'), may hold values from -1.5 to 1.5
- attention_gain: bfloat16 [1280], P('shard'), may hold values from 0.099609375 to 1.8984375
- gate_weight: bfloat16 [1280, 3584], P('shard'), may hold values from -0.15625 to 0.15625
- up_weight: bfloat16 [1280, 3584], P('shard'), may hold values from -0.15625 to 0.15625
- down_weight: bfloat16 [3584, 1280], P(None, 'shard'), may hold values from -0.09375 to 0.09375
- feed_gain: bfloat16 [1280], P('shard'), may hold values from 0.099609375 to 1.8984375
Outputs:
- layer_out: bfloat16 [2, 16384, 1280], P(None, ('rep', 'shard'))
- grad_tokens: bfloat16 [2, 16384, 1280], P(None, ('rep', 'shard'))
- grad_query: float32 [1280, 1280], P('shard')
- grad_key: float32 [1280, 320], P('shard')
- grad_value: float32 [1280, 320], P('shard')
- grad_output: float32 [1280, 1280], P('shard')
- grad_attention_gain: float32 [1280], P('shard')
- grad_gate: float32 [1280, 3584], P('shard')
- grad_up: float32 [1280, 3584], P('shard')
- grad_down: float32 [3584, 1280], P(None, 'shard')
- grad_feed_gain: float32 [1280], P('shard')
Inputs may be any that keep to these rules, and one draw needn't show every extreme that they name: block_map[m, r] names each block of group r's prompt once: entry s is the block that device s of the group holds.
All inputs are finite; a program needn't handle non-finite values.
Results may differ from a plain program's by a relative error of at most 0.023.
Values may be sent and summed in bfloat16 or wider, within the bound.
No kernel may reach another device: no remote copies, remote signals or barrier semaphores. Data moves between devices by JAX's collectives and lax.ppermute only.
A program may use at most 320 MiB of HBM per device.

v0:
```python
import jax
import jax.numpy as jnp
from jax import lax
from jax.experimental import pallas as pl
from jax.experimental.pallas import tpu as pltpu
from jax.sharding import PartitionSpec as P

HEADS = 20
KV_HEADS = 5
HEAD_DIM = 64
GROUP = HEADS // KV_HEADS
EPS = 1e-05
NEG = -1e30
F32 = jnp.float32
BF = jnp.bfloat16
VMEM_BYTES = 62 * 1024 * 1024


def mm(left, right):
    return jnp.dot(left, right, preferred_element_type=F32)


def ein(spec, left, right):
    return jnp.einsum(spec, left, right, preferred_element_type=F32)

def attend_kernel(gap_ref, q_ref, *refs, m, blocks):
    k_ref, v_ref, refs = refs[:blocks], refs[blocks : 2 * blocks], refs[2 * blocks :]
    kl_ref, vl_ref, a_ref, lse_ref = refs
    dim, blk = kl_ref.shape
    keys = jnp.concatenate([k_ref[j][...].T for j in range(blocks)] + [kl_ref[...].T], axis=0)
    ones = jnp.ones((16, (blocks+1)*blk), BF)
    vals = jnp.concatenate([jnp.concatenate([v_ref[j][...] for j in range(blocks)] + [vl_ref[...]], axis=1), ones], axis=0)
    diff = lax.broadcasted_iota(jnp.int32,(blk,blk),0) - lax.broadcasted_iota(jnp.int32,(blk,blk),1)
    n = blocks*blk
    for g in range(GROUP):
        for half in (0,1):
            q = q_ref[g*dim:(g+1)*dim, half*blk:(half+1)*blk]
            if half == 0:
                s = mm(keys[:n], q)
                s = jnp.concatenate([jnp.where(diff <= gap_ref[m, j], s[j*blk:(j+1)*blk], NEG) for j in range(blocks)], axis=0)
                vv = vals[:, :n]
            else:
                s = mm(keys, q)
                s = jnp.concatenate([s[:n], jnp.where(diff <= 0, s[n:], NEG)], axis=0)
                vv = vals
            top = jnp.max(s, axis=0, keepdims=True)
            p = jnp.exp(s - top).astype(BF)
            o = mm(vv, p)
            total = o[dim:dim+1]
            a_ref[g*dim:(g+1)*dim, half*blk:(half+1)*blk] = (o[:dim] / total).astype(BF)
            lse_ref[0, g:g+1, half*blk:(half+1)*blk] = top + jnp.log(total)

def attend(gap, qT, pairs, ownT, micro, m):
    blocks, blk = len(pairs), pairs[0].shape[1]
    rows = qT.shape[1] // micro
    return pl.pallas_call(
        lambda *refs: attend_kernel(*refs, m=m, blocks=blocks),
        grid=(KV_HEADS,),
        in_specs=[
            pl.BlockSpec(memory_space=pltpu.SMEM),
            pl.BlockSpec((GROUP * HEAD_DIM, rows), lambda h: (h, m)),
        ]
        + [pl.BlockSpec((HEAD_DIM, blk), lambda h: (h, 0))] * blocks
        + [pl.BlockSpec((HEAD_DIM, blk), lambda h: (KV_HEADS + h, 0))] * blocks
        + [
            pl.BlockSpec((HEAD_DIM, blk), lambda h: (h, 2 * m + 1)),
            pl.BlockSpec((HEAD_DIM, blk), lambda h: (KV_HEADS + h, 2 * m + 1)),
        ],
        out_specs=[
            pl.BlockSpec((GROUP * HEAD_DIM, rows), lambda h: (h, 0)),
            pl.BlockSpec((1, GROUP, rows), lambda h: (h, 0, 0)),
        ],
        out_shape=[
            jax.ShapeDtypeStruct((qT.shape[0], rows), BF),
            jax.ShapeDtypeStruct((KV_HEADS, GROUP, rows), F32),
        ],
        compiler_params=pltpu.CompilerParams(vmem_limit_bytes=VMEM_BYTES),
        cost_estimate=pl.CostEstimate(flops=3 * 10**10, bytes_accessed=5 * 10**6, transcendentals=12 * 10**6),
        name="attend",
    )(gap, qT, *pairs, *pairs, ownT, ownT)


def back_kernel(gap_ref, cos_ref, sin_ref, kcos_ref, ksin_ref, q_ref, a_ref, da_ref, lse_ref, *refs, m, blocks):
    k_ref, v_ref, refs = refs[:blocks], refs[blocks : 2 * blocks], refs[2 * blocks :]
    kl_ref, vl_ref, dq_ref, terms_ref, own_ref, p_scr, ds_scr = refs
    dim, blk = kl_ref.shape
    n = blocks*blk
    keysT = jnp.concatenate([k_ref[j][...] for j in range(blocks)] + [kl_ref[...]], axis=1)
    keys = jnp.concatenate([k_ref[j][...].T for j in range(blocks)] + [kl_ref[...].T], axis=0)
    vals = jnp.concatenate([v_ref[j][...].T for j in range(blocks)] + [vl_ref[...].T], axis=0)
    diff = lax.broadcasted_iota(jnp.int32,(blk,blk),0) - lax.broadcasted_iota(jnp.int32,(blk,blk),1)
    dk = None; dv = None
    for half in (0,1):
        span = n if half == 0 else n + blk
        cols = slice(half*blk, (half+1)*blk)
        qn = []; dan = []
        for g in range(GROUP):
            rows = slice(g*dim, (g+1)*dim)
            q = q_ref[rows, cols]; da = da_ref[rows, cols]
            qn.append(q.T); dan.append(da.T)
            delta = jnp.sum(da.astype(F32) * a_ref[rows, cols].astype(F32), axis=0, keepdims=True)
            lse = lse_ref[0, g:g+1, cols]
            s = mm(keys[:span], q)
            if half == 0:
                s = jnp.concatenate([jnp.where(diff <= gap_ref[m, j], s[j*blk:(j+1)*blk], NEG) for j in range(blocks)], axis=0)
            else:
                s = jnp.concatenate([s[:n], jnp.where(diff <= 0, s[n:], NEG)], axis=0)
            p = jnp.exp(s - lse)
            dp = mm(vals[:span], da)
            ds = (p * (dp - delta)).astype(BF)
            p_scr[:span, g*blk:(g+1)*blk] = p.astype(BF)
            ds_scr[:span, g*blk:(g+1)*blk] = ds
            dq = mm(keysT[:, :span], ds) * (HEAD_DIM ** -0.5)
            c = cos_ref[:, cols]; sn = sin_ref[:, cols]
            first = dq[:dim//2]; second = dq[dim//2:]
            dq_ref[rows, cols] = jnp.concatenate([first*c + second*sn, second*c - first*sn], axis=0).astype(BF)
        qn = jnp.concatenate(qn, axis=0); dan = jnp.concatenate(dan, axis=0)
        dkh = mm(ds_scr[:span], qn); dvh = mm(p_scr[:span], dan)
        if half == 0:
            dk, dv = dkh, dvh
        else:
            dk = jnp.concatenate([dk + dkh[:n], dkh[n:]], axis=0)
            dv = jnp.concatenate([dv + dvh[:n], dvh[n:]], axis=0)
    half = dim // 2
    for j in range(blocks + 1):
        cols = slice(j * blk, (j + 1) * blk)
        turned = dk[cols].T
        first, second = turned[:half], turned[half:]
        c, sn = kcos_ref[:, cols], ksin_ref[:, cols]
        turned = jnp.concatenate([first * c + second * sn, second * c - first * sn], axis=0).astype(BF)
        value = dv[cols].T.astype(BF)
        if j < blocks:
            terms_ref[j, 0, 0], terms_ref[j, 1, 0] = turned, value
        else:
            own_ref[0, 0], own_ref[1, 0] = turned, value


def attend_back(gap, cosT, sinT, kcos, ksin, qT, aT, daT, lse, pairs, ownT, micro, m, low, high):
    blocks, blk = len(pairs), pairs[0].shape[1]
    rows = qT.shape[1] // micro
    count = high - low
    query = pl.BlockSpec((GROUP * HEAD_DIM, rows), lambda h: (low + h, m))
    part = pl.BlockSpec((GROUP * HEAD_DIM, rows), lambda h: (low + h, 0))
    table = pl.BlockSpec((HEAD_DIM // 2, rows), lambda h: (0, m))
    keys = pl.BlockSpec((HEAD_DIM // 2, (blocks + 1) * blk), lambda h: (0, m))
    return pl.pallas_call(
        lambda *refs: back_kernel(*refs, m=m, blocks=blocks),
        grid=(count,),
        in_specs=[
            pl.BlockSpec(memory_space=pltpu.SMEM),
            table,
            table,
            keys,
            keys,
            query,
            part,
            part,
            pl.BlockSpec((1, GROUP, rows), lambda h: (low + h, 0, 0)),
        ]
        + [pl.BlockSpec((HEAD_DIM, blk), lambda h: (low + h, 0))] * blocks
        + [pl.BlockSpec((HEAD_DIM, blk), lambda h: (KV_HEADS + low + h, 0))] * blocks
        + [
            pl.BlockSpec((HEAD_DIM, blk), lambda h: (low + h, 2 * m + 1)),
            pl.BlockSpec((HEAD_DIM, blk), lambda h: (KV_HEADS + low + h, 2 * m + 1)),
        ],
        out_specs=[
            pl.BlockSpec((GROUP * HEAD_DIM, rows), lambda h: (h, 0)),
            pl.BlockSpec((blocks, 2, 1, HEAD_DIM, blk), lambda h: (0, 0, h, 0, 0)),
            pl.BlockSpec((2, 1, HEAD_DIM, blk), lambda h: (0, h, 0, 0)),
        ],
        out_shape=[
            jax.ShapeDtypeStruct((count * GROUP * HEAD_DIM, rows), BF),
            jax.ShapeDtypeStruct((blocks, 2, count, HEAD_DIM, blk), BF),
            jax.ShapeDtypeStruct((2, count, HEAD_DIM, blk), BF),
        ],
        scratch_shapes=[pltpu.VMEM(((blocks + 1) * blk, GROUP * blk), BF)] * 2,
        compiler_params=pltpu.CompilerParams(vmem_limit_bytes=VMEM_BYTES),
        cost_estimate=pl.CostEstimate(flops=8 * 10**9 * count, bytes_accessed=10**6 * count, transcendentals=0),
        name="attend_back",
    )(gap, cosT, sinT, kcos, ksin, qT, aT, daT, lse, *pairs, *pairs, ownT, ownT)


def nt(left, right):
    return lax.dot_general(left, right, (((1,), (1,)), ((), ())), preferred_element_type=F32)


def tn(left, right):
    return lax.dot_general(left, right, (((0,), (0,)), ((), ())), preferred_element_type=F32)


def project_kernel(row_ref, ht_ref, cos_ref, sin_ref, *refs, pieces, turned, scale):
    parts, (out_ref, whole_ref) = refs[:pieces], refs[pieces:]
    for i, part in enumerate(parts):
        whole_ref[pl.ds(pl.multiple_of(row_ref[i], 16), part.shape[0]), :] = part[...]
    raw = tn(whole_ref[...], ht_ref[...])
    half = HEAD_DIM // 2
    for head in range(raw.shape[0] // HEAD_DIM):
        at = head * HEAD_DIM
        if head < turned:
            first, second = raw[at : at + half], raw[at + half : at + HEAD_DIM]
            cosine, sine = cos_ref[...], sin_ref[...]
            out_ref[at : at + half] = (first * cosine - second * sine).astype(BF) * BF(scale)
            out_ref[at + half : at + HEAD_DIM] = (second * cosine + first * sine).astype(BF) * BF(scale)
        else:
            out_ref[at : at + HEAD_DIM] = raw[at : at + HEAD_DIM].astype(BF)


def project(starts, ht, cosine, sine, pieces, tile, turned, scale):
    width, tokens = ht.shape
    count = pieces[0].shape[1]
    table = pl.BlockSpec(cosine.shape, lambda i: (0, 0))
    return pl.pallas_call(
        lambda *refs: project_kernel(*refs, pieces=len(pieces), turned=turned, scale=scale),
        grid=(count // tile,),
        in_specs=[
            pl.BlockSpec(memory_space=pltpu.SMEM),
            pl.BlockSpec((width, tokens), lambda i: (0, 0)),
            table,
            table,
        ]
        + [pl.BlockSpec((piece.shape[0], tile), lambda i: (0, i)) for piece in pieces],
        out_specs=[
            pl.BlockSpec((tile, tokens), lambda i: (i, 0)),
            pl.BlockSpec((width, tile), lambda i: (0, i)),
        ],
        out_shape=[
            jax.ShapeDtypeStruct((count, tokens), BF),
            jax.ShapeDtypeStruct((width, count), BF),
        ],
        compiler_params=pltpu.CompilerParams(vmem_limit_bytes=VMEM_BYTES),
        cost_estimate=pl.CostEstimate(
            flops=2 * tokens * width * count, bytes_accessed=6 * width * count, transcendentals=0
        ),
        name="project",
    )(starts, ht, cosine, sine, *pieces)


def feed_kernel(row_ref, left_ref, *refs, sets, pieces, groups, split, step):
    hs, cs, refs = refs[:sets], refs[sets : 2 * sets], refs[2 * sets :]
    parts, refs = refs[:pieces], refs[pieces:]
    count = groups * len(split)
    grads, refs = refs[:count], refs[count:]
    backs, refs = refs[:sets], refs[sets:]
    hid_ref, down_ref, ht_ref, ct_ref, gate_ref, up_ref, dg_ref, dw_ref, acc_ref = refs
    tokens, width = hs[0].shape
    at = pl.program_id(0)

    @pl.when(at == 0)
    def _():
        for i in range(sets):
            ht_ref[:, i * tokens : (i + 1) * tokens] = hs[i][...].T
            ct_ref[:, i * tokens : (i + 1) * tokens] = cs[i][...].T
        acc_ref[...] = jnp.zeros_like(acc_ref)

    for k, whole in enumerate((gate_ref, up_ref, down_ref)):
        for i, part in enumerate(parts):
            whole[pl.ds(pl.multiple_of(row_ref[i], 16), part.shape[1]), :] = part[k]
    for i in range(sets):
        for b in range(0, tokens, step):
            rows, to = pl.ds(b, step), pl.ds(i * tokens + b, step)
            gate = mm(hs[i][rows, :], gate_ref[...])
            upper = mm(hs[i][rows, :], up_ref[...])
            grad = mm(cs[i][rows, :], down_ref[...])
            sigma = jax.nn.sigmoid(gate)
            silu = gate * sigma
            hid_ref[to, :] = (silu * upper).astype(BF)
            dg_ref[to, :] = (grad * upper * (sigma + silu * (1.0 - sigma))).astype(BF)
            dw_ref[to, :] = (grad * silu).astype(BF)
    times = ((ht_ref, dg_ref), (ht_ref, dw_ref), (ct_ref, hid_ref))
    for i in range(groups):
        for j, names in enumerate(split):
            out = grads[i * len(split) + j]
            rows = pl.ds(pl.multiple_of(left_ref[i], 16), out.shape[1])
            for at_name, name in enumerate(names):
                left, right = times[name]
                out[at_name] = mm(left[rows, :], right[...]).astype(BF)
    for b in range(0, sets * tokens, step):
        rows = pl.ds(b, step)
        acc_ref[rows, :] += nt(dg_ref[rows, :], gate_ref[...]) + nt(dw_ref[rows, :], up_ref[...])

    @pl.when(at == pl.num_programs(0) - 1)
    def _():
        for i, back in enumerate(backs):
            back[...] = acc_ref[pl.ds(i * tokens, tokens), :].astype(BF)


def feed(starts, left_starts, hs, cs, parts, sizes, rows, split=((0, 1, 2),), tile=256, step=256):
    sets = len(hs)
    tokens, width = rows, hs[0][0].shape[1]
    hidden = parts[0].shape[2]
    one = pl.Buffered(1)
    back = pl.BlockSpec((tokens, width), lambda i: (0, 0), pipeline_mode=one)
    toks = [pl.BlockSpec((tokens, width), lambda i, at=at: (at, 0), pipeline_mode=one) for _, at in hs + cs]
    smem = pl.BlockSpec(memory_space=pltpu.SMEM)
    counts = [(len(names), size) for size in sizes for names in split]
    grad_specs = [pl.BlockSpec((count, size, tile), lambda i: (0, 0, i)) for count, size in counts]
    grad_shapes = [jax.ShapeDtypeStruct((count, size, hidden), BF) for count, size in counts]
    results = pl.pallas_call(
        lambda *refs: feed_kernel(*refs, sets=sets, pieces=len(parts), groups=len(sizes), split=split, step=step),
        grid=(hidden // tile,),
        in_specs=[smem, smem]
        + toks
        + [pl.BlockSpec((3, part.shape[1], tile), lambda i: (0, 0, i)) for part in parts],
        out_specs=grad_specs
        + [back] * sets
        + [pl.BlockSpec((sets * tokens, tile), lambda i: (0, i)), pl.BlockSpec((width, tile), lambda i: (0, i))],
        out_shape=grad_shapes
        + [jax.ShapeDtypeStruct((tokens, width), BF)] * sets
        + [jax.ShapeDtypeStruct((sets * tokens, hidden), BF), jax.ShapeDtypeStruct((width, hidden), BF)],
        scratch_shapes=[pltpu.VMEM((width, sets * tokens), BF)] * 2
        + [pltpu.VMEM((width, tile), BF)] * 2
        + [pltpu.VMEM((sets * tokens, tile), BF)] * 2
        + [pltpu.VMEM((sets * tokens, width), F32)],
        compiler_params=pltpu.CompilerParams(vmem_limit_bytes=VMEM_BYTES),
        cost_estimate=pl.CostEstimate(
            flops=16 * sets * tokens * width * hidden,
            bytes_accessed=14 * width * hidden + 12 * sets * tokens * width,
            transcendentals=sets * tokens * hidden,
        ),
        name="feed",
    )(starts, left_starts, *[h for h, _ in hs], *[c for c, _ in cs], *parts)
    count = len(grad_specs)
    return results[:count], results[count : count + sets], results[-2], results[-1]


def prepare_kernel(x_ref, gain_ref, ht_ref):
    source = x_ref[...].astype(F32)
    scale = lax.rsqrt(jnp.mean(source * source, axis=-1, keepdims=True) + EPS)
    ht_ref[...] = (source * scale * gain_ref[...]).astype(BF).T


def prepare(x, gain, tile=256):
    tokens, width = x.shape
    return pl.pallas_call(
        prepare_kernel,
        grid=(tokens // tile,),
        in_specs=[pl.BlockSpec((tile, width), lambda i: (i, 0)), pl.BlockSpec((1, width), lambda i: (0, 0))],
        out_specs=pl.BlockSpec((width, tile), lambda i: (0, i)),
        out_shape=jax.ShapeDtypeStruct((width, tokens), BF),
        compiler_params=pltpu.CompilerParams(vmem_limit_bytes=VMEM_BYTES),
        cost_estimate=pl.CostEstimate(flops=0, bytes_accessed=6 * 10**6, transcendentals=0),
        name="prepare",
    )(x, gain)


def merge_kernel(row_ref, at_ref, x_ref, gain_ref, *refs, pieces):
    if pieces == 1:
        whole_ref, mid_ref, h_ref = refs
    else:
        parts, (mid_ref, h_ref, whole_ref) = refs[:pieces], refs[pieces:]
        for i, part in enumerate(parts):
            whole_ref[pl.ds(pl.multiple_of(row_ref[i], 16), part.shape[0]), :] = part[...]
    middle = x_ref[...].astype(F32) + tn(at_ref[...], whole_ref[...])
    scale = lax.rsqrt(jnp.mean(middle * middle, axis=-1, keepdims=True) + EPS)
    mid_ref[...] = middle
    h_ref[...] = (middle * scale * gain_ref[...]).astype(BF)


def merge(starts, at, x, m, gain, pieces):
    head_width, tokens = at.shape
    width = x.shape[1]
    row = pl.BlockSpec((tokens, width), lambda i: (0, 0))
    outs = [row, row]
    shapes = [jax.ShapeDtypeStruct((tokens, width), F32), jax.ShapeDtypeStruct((tokens, width), BF)]
    if len(pieces) > 1:
        outs.append(pl.BlockSpec((head_width, width), lambda i: (0, 0)))
        shapes.append(jax.ShapeDtypeStruct((head_width, width), BF))
    return pl.pallas_call(
        lambda *refs: merge_kernel(*refs, pieces=len(pieces)),
        grid=(1,),
        in_specs=[
            pl.BlockSpec(memory_space=pltpu.SMEM),
            pl.BlockSpec((head_width, tokens), lambda i: (0, 0)),
            pl.BlockSpec((tokens, width), lambda i: (m, 0)),
            pl.BlockSpec((1, width), lambda i: (0, 0)),
        ]
        + [pl.BlockSpec(piece.shape, lambda i: (0, 0)) for piece in pieces],
        out_specs=outs,
        out_shape=shapes,
        compiler_params=pltpu.CompilerParams(vmem_limit_bytes=VMEM_BYTES),
        cost_estimate=pl.CostEstimate(
            flops=2 * tokens * width * head_width, bytes_accessed=16 * 10**6, transcendentals=0
        ),
        name="merge",
    )(starts, at, x, gain, *pieces)


def unmerge_kernel(mid_ref, c_ref, gain_ref, whole_ref, *refs):
    backs, (dmid_ref, da_ref) = refs[:-2], refs[-2:]
    middle = mid_ref[...]
    scale = lax.rsqrt(jnp.mean(middle * middle, axis=-1, keepdims=True) + EPS)
    unit = middle * scale
    grad = backs[0][...].astype(F32)
    for back in backs[1:]:
        grad = grad + back[...].astype(F32)
    weighted = grad * gain_ref[...]
    mean = jnp.mean(weighted * unit, axis=-1, keepdims=True)
    dmid = (c_ref[...].astype(F32) + scale * (weighted - unit * mean)).astype(BF)
    dmid_ref[...] = dmid
    da_ref[...] = nt(whole_ref[...], dmid).astype(BF)


def unmerge(mid, c, m, gain, whole, backs, tile=256):
    tokens, width = mid.shape
    head_width = whole.shape[0]
    row = pl.BlockSpec((tile, width), lambda i: (i, 0))
    return pl.pallas_call(
        unmerge_kernel,
        grid=(tokens // tile,),
        in_specs=[
            row,
            pl.BlockSpec((tile, width), lambda i: (m * (tokens // tile) + i, 0)),
            pl.BlockSpec((1, width), lambda i: (0, 0)),
            pl.BlockSpec((head_width, width), lambda i: (0, 0)),
        ]
        + [row] * len(backs),
        out_specs=[row, pl.BlockSpec((head_width, tile), lambda i: (0, i))],
        out_shape=[
            jax.ShapeDtypeStruct((tokens, width), BF),
            jax.ShapeDtypeStruct((head_width, tokens), BF),
        ],
        compiler_params=pltpu.CompilerParams(vmem_limit_bytes=VMEM_BYTES),
        cost_estimate=pl.CostEstimate(
            flops=2 * tokens * width * head_width, bytes_accessed=16 * 10**6, transcendentals=0
        ),
        name="unmerge",
    )(mid, c, gain, whole, *backs)


def terms_kernel(left_ref, *refs, count, turned):
    lefts, rights, outs = refs[:count], refs[count : 2 * count], refs[2 * count :]
    times = nt if turned else mm
    for i, out in enumerate(outs):
        rows = pl.ds(pl.multiple_of(left_ref[i], 16), out.shape[0])
        total = times(lefts[0][rows, :], rights[0][...])
        for left, right in zip(lefts[1:], rights[1:]):
            total = total + times(left[rows, :], right[...])
        out[...] = total.astype(BF)


def grad_terms(left_starts, lefts, rights, turned, size, tile):
    columns = rights[0].shape[0 if turned else 1]
    span = rights[0].shape[1 if turned else 0]
    count = left_starts.shape[0]
    if turned:
        right_specs = [pl.BlockSpec((tile, span), lambda i: (i, 0)) for _ in rights]
    else:
        right_specs = [pl.BlockSpec((span, tile), lambda i: (0, i)) for _ in rights]
    left_specs = [pl.BlockSpec((left.shape[0], span), lambda i, at=at: (0, at)) for left, at in lefts]
    return pl.pallas_call(
        lambda *refs: terms_kernel(*refs, count=len(lefts), turned=turned),
        grid=(columns // tile,),
        in_specs=[pl.BlockSpec(memory_space=pltpu.SMEM)] + left_specs + right_specs,
        out_specs=[pl.BlockSpec((size, tile), lambda i: (0, i))] * count,
        out_shape=[jax.ShapeDtypeStruct((size, columns), BF)] * count,
        compiler_params=pltpu.CompilerParams(vmem_limit_bytes=VMEM_BYTES),
        cost_estimate=pl.CostEstimate(
            flops=2 * len(lefts) * span * columns * size * count, bytes_accessed=8 * 10**6, transcendentals=0
        ),
        name="grad_terms",
    )(left_starts, *[left for left, _ in lefts], *rights)


def joint_kernel(left_ref, *refs, plan, sizes, outs):
    refs, outs = refs[:-outs], refs[-outs:]
    for i, out in enumerate(outs):
        rows = pl.ds(pl.multiple_of(left_ref[i], 16), out.shape[0])
        column = 0
        for steps, count in zip(plan, sizes):
            total = 0.0
            for left, at, right, index in steps:
                value = refs[right][...] if index is None else refs[right][index]
                total = total + nt(refs[left][rows, at : at + value.shape[1]], value)
            out[:, column : column + count] = total.astype(BF)
            column += count


def joint_terms(left_starts, arrays, plan, sizes, size):
    whole = [pl.BlockSpec(array.shape, lambda i, n=array.ndim: (0,) * n) for array in arrays]
    outs = left_starts.shape[0]
    return pl.pallas_call(
        lambda *refs: joint_kernel(*refs, plan=plan, sizes=sizes, outs=outs),
        grid=(1,),
        in_specs=[pl.BlockSpec(memory_space=pltpu.SMEM)] + whole,
        out_specs=[pl.BlockSpec((size, sum(sizes)), lambda i: (0, 0))] * outs,
        out_shape=[jax.ShapeDtypeStruct((size, sum(sizes)), BF)] * outs,
        compiler_params=pltpu.CompilerParams(vmem_limit_bytes=VMEM_BYTES),
        cost_estimate=pl.CostEstimate(flops=6 * 10**9, bytes_accessed=14 * 10**6, transcendentals=0),
        name="joint_terms",
    )(left_starts, *arrays)


def output_kernel(*refs, parts, adds, firsts):
    hids, downs, refs = refs[:parts], refs[parts : 2 * parts], refs[2 * parts :]
    adds, firsts, out_ref = refs[:adds], refs[adds:-1], refs[-1]
    total = nt(hids[0][...], downs[0][...])
    for hid, down in zip(hids[1:], downs[1:]):
        total = total + nt(hid[...], down[...])
    for add in adds:
        total = total + add[...].astype(F32)
    if not firsts:
        out_ref[...] = total.astype(BF)
    for i, first in enumerate(firsts):

        @pl.when(pl.program_id(0) == i)
        def _():
            out_ref[...] = (total + first[...]).astype(BF)


def output(hids, downs, adds, firsts, skip, tile):
    width = downs[0].shape[0]
    row = pl.BlockSpec((tile, width), lambda i: (i, 0))
    return pl.pallas_call(
        lambda *refs: output_kernel(*refs, parts=len(hids), adds=len(adds), firsts=len(firsts)),
        grid=(2,),
        in_specs=[pl.BlockSpec((tile, hid.shape[1]), lambda i: (skip + i, 0)) for hid in hids]
        + [pl.BlockSpec(down.shape, lambda i: (0, 0)) for down in downs]
        + [row] * len(adds)
        + [pl.BlockSpec((tile, width), lambda i: (0, 0))] * len(firsts),
        out_specs=row,
        out_shape=jax.ShapeDtypeStruct((2 * tile, width), BF),
        compiler_params=pltpu.CompilerParams(vmem_limit_bytes=VMEM_BYTES),
        cost_estimate=pl.CostEstimate(flops=5 * 10**9, bytes_accessed=16 * 10**6, transcendentals=0),
        name="output",
    )(*hids, *downs, *adds, *firsts)


def finish_kernel(x_ref, gain_ref, dmid_ref, dq_ref, dp_ref, query_ref, pair_ref, out_ref):
    source = x_ref[...].astype(F32)
    scale = lax.rsqrt(jnp.mean(source * source, axis=-1, keepdims=True) + EPS)
    unit = source * scale
    grad = (mm(query_ref[...], dq_ref[...]) + mm(pair_ref[...], dp_ref[...])).T
    weighted = grad * gain_ref[...]
    mean = jnp.mean(weighted * unit, axis=-1, keepdims=True)
    out_ref[...] = (dmid_ref[...].astype(F32) + scale * (weighted - unit * mean)).astype(BF)


def finish(x, m, gain, dmid, dq, dp, query, pair, tile=256):
    tokens, width = dmid.shape
    row = pl.BlockSpec((tile, width), lambda i: (i, 0))
    return pl.pallas_call(
        finish_kernel,
        grid=(tokens // tile,),
        in_specs=[
            pl.BlockSpec((tile, width), lambda i: (m * (tokens // tile) + i, 0)),
            pl.BlockSpec((1, width), lambda i: (0, 0)),
            row,
            pl.BlockSpec((dq.shape[0], tile), lambda i: (0, i)),
            pl.BlockSpec((dp.shape[0], tile), lambda i: (0, i)),
            pl.BlockSpec(query.shape, lambda i: (0, 0)),
            pl.BlockSpec(pair.shape, lambda i: (0, 0)),
        ],
        out_specs=row,
        out_shape=jax.ShapeDtypeStruct((tokens, width), BF),
        compiler_params=pltpu.CompilerParams(vmem_limit_bytes=VMEM_BYTES),
        cost_estimate=pl.CostEstimate(
            flops=2 * tokens * width * (dq.shape[0] + dp.shape[0]), bytes_accessed=12 * 10**6, transcendentals=0
        ),
        name="finish",
    )(x, gain, dmid, dq, dp, query, pair)


def widen_kernel(core_ref, *refs, parts, counts):
    mine, theirs, refs = refs[:parts], refs[parts : 2 * parts], refs[2 * parts :]
    gate_ref, up_ref, gate_grad, up_grad, down_grad, sums_ref = refs
    step = pl.program_id(0)
    tiles = sum(counts)
    at = step % tiles
    picked = None
    low = 0
    for part, other, count in zip(mine, theirs, counts):
        here = jnp.where(step < tiles, part[...], other[...])
        picked = here if picked is None else jnp.where(at < low, picked, here)
        low += count
    picked = picked.astype(F32)
    gate_grad[...] = picked[0]
    up_grad[...] = picked[1]
    down_grad[...] = picked[2]

    @pl.when(step == 0)
    def _():
        sums_ref[...] = jnp.zeros_like(sums_ref)

    terms = gate_ref[...].astype(F32) * picked[0] + up_ref[...].astype(F32) * picked[1]
    sums_ref[...] += jnp.sum(terms, axis=1, keepdims=True)


def widen(core, mine, theirs, gate, up, tile=256):
    rows, hidden = gate.shape
    counts = [part.shape[2] // tile for part in mine]
    tiles = sum(counts)
    lows = [sum(counts[:i]) for i in range(len(counts))]

    def place(step, core):
        return (core[0] ^ (step // tiles)) * tiles + step % tiles

    def inside(step, low, count):
        return jnp.minimum(jnp.maximum(step - low, 0), count - 1)

    mine_specs = [
        pl.BlockSpec((3, rows, tile), lambda i, core, low=low, count=count: (0, 0, inside(i, low, count)))
        for low, count in zip(lows, counts)
    ]
    their_specs = [
        pl.BlockSpec((3, rows, tile), lambda i, core, low=low, count=count: (0, 0, inside(i - tiles, low, count)))
        for low, count in zip(lows, counts)
    ]
    wide = pl.BlockSpec((rows, tile), lambda i, core: (0, place(i, core)))
    return pl.pallas_call(
        lambda *refs: widen_kernel(*refs, parts=len(mine), counts=counts),
        grid_spec=pltpu.PrefetchScalarGridSpec(
            num_scalar_prefetch=1,
            grid=(2 * tiles,),
            in_specs=mine_specs + their_specs + [wide, wide],
            out_specs=[wide, wide, wide, pl.BlockSpec((rows, 1), lambda i, core: (0, 0))],
        ),
        out_shape=[
            jax.ShapeDtypeStruct((rows, hidden), F32),
            jax.ShapeDtypeStruct((rows, hidden), F32),
            jax.ShapeDtypeStruct((rows, hidden), F32),
            jax.ShapeDtypeStruct((rows, 1), F32),
        ],
        compiler_params=pltpu.CompilerParams(vmem_limit_bytes=VMEM_BYTES),
        cost_estimate=pl.CostEstimate(flops=0, bytes_accessed=26 * 10**6, transcendentals=0),
        name="widen",
    )(core, *mine, *theirs, gate, up)


def partner(value, axis, size, bit):
    return lax.ppermute(value, axis, [(i, i ^ bit) for i in range(size)])


def after(value, *others):
    return lax.optimization_barrier((value,) + others)[0]


def pick(value, index, axis):
    return lax.dynamic_index_in_dim(value, index, axis, keepdims=False)


def pair_up(mine, other, index, axis):
    first = jnp.where(index == 0, mine, other)
    second = jnp.where(index == 0, other, mine)
    return jnp.stack([first, second], axis=axis)


class Fast:
    chip = 2

    def __init__(self, rows):
        self.rows = rows
        member, rep = lax.axis_index("shard"), lax.axis_index("rep")
        self.member, self.rep_index = member, rep
        self.c, self.y, self.z, self.far = member % 2, rep % 2, (rep // 2) % 2, rep // 4
        self.order = [member, member ^ 2, member ^ 1, member ^ 3]
        across = member // 2
        self.feed_starts = jnp.stack([across * 2 * rows, (1 - across) * 2 * rows]).astype(jnp.int32)
        self.feed_sizes = (2 * rows, 2 * rows)
        self.starts = jnp.stack([which * rows for which in self.order]).astype(jnp.int32)
        self.left_starts = self.feed_starts

    def x(self, value):
        return partner(value, "shard", 4, 2)

    def core(self, value):
        return partner(value, "shard", 4, 1)

    def rep(self, value, bit):
        return partner(value, "rep", 8, bit)

    def pieces(self, value, behind=None):
        across = self.x(value)
        return [value, across, self.core(value), self.core(across)]


    def feed_columns(self, columns):
        return self.c * (columns // 2), columns // 2

    def feed_core(self, shards, low, high, columns):
        half = columns // 2

        def cut(which):
            return jnp.stack([lax.dynamic_slice_in_dim(s, which * half + low, high - low, 1) for s in shards])

        mine, theirs = cut(self.c), cut(1 - self.c)
        both = pair_up(mine, self.core(theirs), self.c, 1)
        return both.reshape(3, 2 * self.rows, high - low)

    def feed_eighth(self, both):
        flat = both.reshape(-1, both.shape[2])
        eighth = flat.shape[0] // 8
        return self.x(lax.dynamic_slice_in_dim(flat, self.rep_index * eighth, eighth, 0))

    def feed_parts(self, both, eighth):
        return [both, self.spread(eighth).reshape(both.shape)]

    def gather_pairs(self, sent):
        both = jnp.stack([sent, self.x(sent)])
        return jnp.concatenate([both, self.core(both)], axis=0)

    def spread(self, eighth):
        return lax.all_gather(eighth, "rep", axis=0, tiled=True)

    def z_sum(self, value, order=(0, 1)):
        lines = [[at for at in range(8) if at % 2 == y] for y in order]
        return lax.psum(value, "rep", axis_index_groups=lines)

    def deal(self, held):
        first, second = [], []
        for at in range(32):
            rep, member = at // 4, at % 4
            y, c = rep % 2, member % 2
            here, there = rep * 4 + member - c + y, (rep ^ 1) * 4 + member - c + y
            if c == y:
                first.append((at, there))
            else:
                first.append((at, here))
                second.append((at, there))
        return [lax.ppermute(held, ("rep", "shard"), pairs) for pairs in (first, second)]

    def dealt(self, held, got):
        stay = self.c == self.y
        return jnp.where(stay, held, got[0]), jnp.where(stay, got[0], got[1])


class Chain:
    def __init__(self, net, kept, outward, count=1):
        self.net, self.stage, self.got = net, 0, None
        self.shape = (count, 2, kept.shape[0] // (2 * count), kept.shape[1])
        self.parts, self.out = [kept], outward

    def total(self):
        return sum(part.astype(F32) for part in self.parts + [self.got]).astype(BF)

    def ready(self):
        if self.stage == 1:
            parts = [part.reshape(self.shape) for part in self.parts + [self.got]]
            y = self.net.y
            self.out = sum(pick(part, 1 - y, 1).astype(F32) for part in parts).astype(BF)
            self.parts = [pick(part, y, 1) for part in parts]
        elif self.stage > 1:
            self.out = self.total()
            self.parts = [self.out]
        return self.out

    def move(self):
        if self.stage == 0:
            self.got = self.net.x(self.out)
        else:
            self.got = self.net.rep(self.out, (1, 2, 4)[self.stage - 1])
        self.stage += 1


def settle(chains, *others):
    values = lax.optimization_barrier(tuple(chain.got for chain in chains) + others)
    for chain, value in zip(chains, values):
        chain.got = value
    return values[len(chains) :]


def advance(chains, *others):
    outs = [chain.ready() for chain in chains]
    values = lax.optimization_barrier(tuple(outs) + others)
    for chain, value in zip(chains, values):
        chain.out = value
        chain.move()
    return values[len(chains) :]


class General:
    chip = 1

    def __init__(self, rows):
        shards = lax.axis_size("shard")
        self.rows, self.shards = rows, shards
        self.member = lax.axis_index("shard")
        self.order = [jnp.int32(i) for i in range(shards)]
        self.starts = jnp.arange(shards, dtype=jnp.int32) * rows
        self.feed_starts = self.starts
        self.left_starts = jnp.zeros((1,), jnp.int32)
        self.feed_sizes = (shards * rows,)

    def pieces(self, value):
        whole = lax.all_gather(value, "shard", axis=0)
        return [whole[i] for i in range(self.shards)]

    def feed_core(self, shards, low, high, columns):
        return jnp.stack([shard[:, low:high] for shard in shards])

    def gather_pairs(self, sent):
        return lax.all_gather(sent, "shard", axis=0)

    def sum_pairs(self, terms):
        return lax.psum_scatter(terms, "shard", scatter_dimension=0, tiled=False).astype(F32)

    def whole_sum(self, terms, axis):
        owned = lax.psum_scatter(terms, "shard", scatter_dimension=axis, tiled=True)
        return lax.psum(owned, "rep").astype(F32)


def on_device(
    tokens,
    cotangent,
    block_map,
    query_weight,
    key_weight,
    value_weight,
    output_weight,
    attention_gain,
    gate_weight,
    up_weight,
    down_weight,
    feed_gain,
):
    shards = lax.axis_size("shard")
    fast = shards == 4 and lax.axis_size("rep") == 8
    micro, rows, width = tokens.shape
    block = rows // 2
    total = micro * rows
    shard_rows = query_weight.shape[0]
    net = Fast(shard_rows) if fast else General(shard_rows)
    head_width = HEADS * HEAD_DIM
    pair_width = KV_HEADS * HEAD_DIM
    hidden_width = gate_weight.shape[1]
    batches = range(micro)

    gain_pieces = net.pieces(jnp.stack([attention_gain, feed_gain], axis=1))
    gains = jnp.zeros((width, 2), BF)
    for i, piece in enumerate(gain_pieces):
        gains = lax.dynamic_update_slice_in_dim(gains, piece, net.starts[i], 0)
    gain_one = gains[:, 0].astype(F32)[None, :]
    gain_two = gains[:, 1].astype(F32)[None, :]
    pair_pieces = net.pieces(jnp.concatenate([key_weight, value_weight], axis=1))
    feed_shards = [gate_weight, up_weight, down_weight.T]
    columns = hidden_width // net.chip
    cuts = [0, 512, 1280, columns] if fast else [0, columns]

    blocks_here = block_map[:, 0]
    own_block = lax.dynamic_index_in_dim(blocks_here, net.member, axis=1, keepdims=False)
    others = jnp.stack(
        [lax.dynamic_index_in_dim(blocks_here, which, axis=1, keepdims=False) for which in net.order],
        axis=1,
    )
    gap = ((own_block[:, None] - others) * block).astype(jnp.int32)
    inside = jnp.arange(block, dtype=jnp.int32)
    place = jnp.concatenate(
        [
            own_block[:, None] * block + inside[None, :],
            jnp.broadcast_to(block * shards + inside[None, :], (micro, block)),
        ],
        axis=1,
    ).reshape(total)
    half = HEAD_DIM // 2
    freq = jnp.exp(jnp.arange(half, dtype=F32) * (-2.0 * jnp.log(10000.0) / HEAD_DIM))
    angle = freq[:, None] * place.astype(F32)[None, :]
    cosine, sine = jnp.cos(angle), jnp.sin(angle)

    key_place = jnp.concatenate(
        [
            (others[:, :, None] * block + inside).reshape(micro, -1),
            jnp.broadcast_to(block * shards + inside[None, :], (micro, block)),
        ],
        axis=1,
    ).reshape(-1)
    key_angle = freq[:, None] * key_place.astype(F32)[None, :]
    key_cosine, key_sine = jnp.cos(key_angle), jnp.sin(key_angle)

    source = tokens.reshape(total, width)
    turned_one = prepare(source, gain_one)
    upstream = cotangent.reshape(total, width)
    if fast:
        bind = lax.optimization_barrier

        def core_of(part, *others):
            shards_after = [after(shard, *others) if others else shard for shard in feed_shards]
            return net.feed_core(shards_after, cuts[part], cuts[part + 1], hidden_width)

        feed_cores = [core_of(0)]
        query_across = net.x(after(query_weight, pair_pieces[1]))
        pair_across = after(pair_pieces[1], turned_one)
        pair_pieces = [pair_pieces[0], pair_across, pair_pieces[2], net.core(pair_across)]
        own_pairs, pair_full = project(net.starts, turned_one, cosine, sine, pair_pieces, 640, KV_HEADS, 1.0)
        sent = [own_pairs[:, m * rows : m * rows + block] for m in batches]
        across = [net.x(part) for part in sent]
        across[0], turned_q = bind((across[0], turned_one))
        query_across = after(query_across, sent[1])
        query_pieces = [query_weight, query_across, net.core(query_weight), net.core(query_across)]
        pairs = [[sent[0], across[0], net.core(sent[0]), net.core(across[0])]]
        query, query_full = project(net.starts, turned_q, cosine, sine, query_pieces, 640, HEADS, HEAD_DIM**-0.5)
        eighths = [net.feed_eighth(after(part, across[0])) for part in feed_cores]
        moved = net.core(after(upstream, across[0]))
        upstream_all = [(upstream, m) for m in batches] + [(moved, m) for m in batches]
        turned_other = net.core(after(turned_one, across[0]))
        output_across = net.x(after(output_weight, across[0]))
        mixed_0, log_0 = attend(gap, query, pairs[0], own_pairs, micro, 0)
        mixed_0, output_across, across[1], eighth_0 = bind((mixed_0, output_across, across[1], eighths[0]))
        feed_parts = [net.feed_parts(feed_cores[0], eighth_0)]
        pairs.append([sent[1], across[1], net.core(sent[1]), net.core(across[1])])
        feed_cores += [core_of(1, mixed_0), core_of(2, mixed_0)]
        eighth_1, eighth_2 = [net.feed_eighth(part) for part in feed_cores[1:]]
        output_pieces = [output_weight, output_across, net.core(output_weight), net.core(output_across)]
        mixed_1, log_1 = attend(after(gap, mixed_0), query, pairs[1], own_pairs, micro, 1)
        mixed_1, eighth_1, eighth_2 = bind((mixed_1, eighth_1, eighth_2))
        feed_parts += [net.feed_parts(feed_cores[1], eighth_1), net.feed_parts(feed_cores[2], eighth_2)]
        mixed, log_total = [mixed_0, mixed_1], [log_0, log_1]
        mixed_all = mixed + [net.core(value) for value in mixed]
        middle_0, normed_0, output_full = merge(
            net.starts, after(mixed_0, mixed_1), source, 0, gain_two, output_pieces
        )
        middle_1, normed_1 = merge(net.starts, mixed_1, source, 1, gain_two, [output_full])
        middle, normed_two = [middle_0, middle_1], [normed_0, normed_1]
        normed_all = [(value, 0) for value in normed_two] + [(net.core(value), 0) for value in normed_two]
    else:
        own_pairs, pair_full = project(net.starts, turned_one, cosine, sine, pair_pieces, 640, KV_HEADS, 1.0)
        pairs = [list(net.gather_pairs(own_pairs[:, m * rows : m * rows + block])) for m in batches]
        query_pieces = net.pieces(query_weight)
        query, query_full = project(net.starts, turned_one, cosine, sine, query_pieces, 640, HEADS, HEAD_DIM**-0.5)
        feed_parts = [net.pieces(jnp.stack(feed_shards))]
        output_pieces = net.pieces(output_weight)
        mixed, log_total, middle, normed_two = [], [], [], []
        for m in batches:
            mixed_m, log_m = attend(gap, query, pairs[m], own_pairs, micro, m)
            middle_m, normed_m, output_full = merge(net.starts, mixed_m, source, m, gain_two, output_pieces)
            mixed.append(mixed_m)
            log_total.append(log_m)
            middle.append(middle_m)
            normed_two.append(normed_m)
        normed_all = [(value, 0) for value in normed_two]
        upstream_all = [(upstream, m) for m in batches]

    backs = [[] for _ in batches]
    hids, downs, feed_terms, ones = [], [], [], []
    starts = net.feed_starts
    for k, parts in enumerate(feed_parts):
        split = ((0, 1), (2,)) if fast and k == 1 else ((0, 1, 2),)
        grads, backs_here, hid, down = feed(
            starts, net.left_starts, normed_all, upstream_all, parts, net.feed_sizes, rows, split
        )
        feed_terms.append(grads)
        if fast and k == 2:
            settled = settle(ones[:2], *backs_here, hid)
            backs_here, hid = settled[:-1], settled[-1]
        for m in batches:
            backs[m].append(backs_here[m])
            if fast:
                backs[m].append(net.core(backs_here[micro + m]))
        if fast:
            grads = [grad.reshape(-1, grad.shape[-1]) for grad in grads]
            ones += [Chain(net, grads[j], grads[len(split) + j], len(names)) for j, names in enumerate(split)]
        hids.append(hid)
        downs.append(down)
        starts = after(net.feed_starts, hid)
        if fast and k == 0:
            prompt = jnp.concatenate(
                [turned_one[:, m * rows : m * rows + block] for m in batches], axis=1
            )
            prompt_across = net.x(after(prompt, normed_two[-1]))
            starts, prompt_across = bind((starts, prompt_across))
            prompts = [prompt, prompt_across, net.core(prompt), net.core(prompt_across)]
            ones[0].move()
        elif fast and k == 1:
            (starts,) = settle(ones[:1], starts)
            (starts,) = advance(ones[:1], starts)
            ones[1].move()
    size = net.feed_sizes[0]

    def back_of(m, grad_mixed, low, high):
        return attend_back(
            gap, cosine, sine, key_cosine, key_sine, query, mixed[m], grad_mixed, log_total[m], pairs[m], own_pairs, micro, m, low, high
        )

    def pair_grads(summed, own_terms):
        return jnp.concatenate([summed.astype(BF), own_terms], axis=-1).reshape(2 * pair_width, rows)

    def finish_of(m, dmid, grad_query, grad_pairs):
        return finish(source, m, gain_one, dmid, grad_query, grad_pairs, query_full, pair_full)

    if fast:
        lefts_one = [(turned_one, 0), (turned_one, 1), (turned_other, 0), (turned_other, 1)]
        lefts_mixed = [(value, 0) for value in mixed_all]
        part_1, part_2, part_3, part_4 = ones

        def split(value, axis):
            size = value.shape[axis] // 2
            return [lax.dynamic_slice_in_dim(value, at * size, size, axis) for at in (net.c, 1 - net.c)]

        middle_0, first = advance([part_2, part_3], after(middle[0], backs[0][-1]), part_1.total())
        first = net.z_sum(first)
        def kind(value, which):
            return lax.dynamic_index_in_dim(value, which, value.ndim - 4, keepdims=False)

        def pairs_out(terms, own):
            extra = jnp.concatenate([kind(terms[:2], 1 - net.c), kind(own, 1 - net.c)[None]], axis=0)
            return net.core(terms[2:]), net.core(extra)

        def pairs_chip(terms, own, away, extra):
            mine = kind(terms, net.c).astype(F32)
            theirs = jnp.concatenate([kind(away, net.c), extra[:2]], axis=0).astype(F32)
            return (mine + theirs).astype(BF).reshape(4, pair_width, block), [
                value.reshape(pair_width, block) for value in (kind(own, net.c), extra[2])
            ]

        dmid_0, mixed_0 = unmerge(middle_0, upstream, 0, gain_two, output_full, backs[0])
        theirs = output(hids, [downs[0], downs[1], after(downs[2], mixed_0)], [], [], micro, rows)
        mixed_0, theirs = settle([part_2, part_3], mixed_0, theirs)
        theirs = net.core(theirs)
        (mixed_0,) = advance([part_3, part_4], mixed_0)
        query_0, terms_0, own_0 = back_of(0, mixed_0, 0, KV_HEADS)
        query_0, terms_0, theirs, first = settle([part_3], query_0, terms_0, theirs, first)
        away_0, extra_0 = pairs_out(terms_0, own_0)
        second = jnp.concatenate([part_2.total(), part_3.total()], axis=0)
        halves_0 = split(after(dmid_0, query_0), 1)
        second, middle_1 = bind((second, after(middle[1], query_0)))
        second = net.z_sum(second)
        dmid_1, mixed_1 = unmerge(middle_1, upstream, 1, gain_two, output_full, backs[1])
        halves_1 = split(dmid_1, 1)
        mixed_1, moved_0, moved_1, away_0, extra_0 = settle(
            [part_4], mixed_1, halves_0[1], halves_1[1], away_0, extra_0
        )
        kept_0 = (terms_0[:2].astype(F32) + away_0.astype(F32)).astype(BF)
        mixed_1, moved_0, moved_1, out_0 = advance([part_4], mixed_1, moved_0, moved_1, kept_0[1])
        got_0 = net.x(out_0)
        dmid_halves = [halves_0[0], halves_1[0], net.core(moved_0), net.core(moved_1)]
        query_1, terms_1, own_1 = back_of(1, mixed_1, 0, 3)
        output_terms = grad_terms(
            net.left_starts, lefts_mixed, [after(value, query_1) for value in dmid_halves], False, size, 640
        )

        query_1, got_0, *output_terms = settle([part_4], query_1, got_0, *output_terms)
        blocks_0, owns_0 = pairs_chip(terms_0, own_0, away_0, extra_0)
        chain_o = Chain(net, *output_terms)
        mixed_1, third, blocks_0 = advance([chain_o], after(mixed_1, query_1), part_4.total(), blocks_0)
        third = net.z_sum(third, (1, 0))
        got_1st = net.deal(after(first, mixed_1))
        query_1b, terms_1b, own_1b = back_of(1, mixed_1, 3, KV_HEADS)

        query_1b, second = settle([chain_o], query_1b, second)
        terms_1 = jnp.concatenate([terms_1, terms_1b], axis=2)
        own_1 = jnp.concatenate([own_1, own_1b], axis=1)
        grad_query = [query_0, jnp.concatenate([query_1, query_1b], axis=0)]
        halves = [split(value, 0) for value in grad_query]
        moved_0, moved_1, terms_1 = bind((halves[0][1], halves[1][1], terms_1))
        away_1, extra_1 = pairs_out(terms_1, own_1)
        query_halves = [halves[0][0], halves[1][0], net.core(moved_0), net.core(moved_1)]
        (out_o,) = bind((chain_o.ready(),))
        away_1, extra_1, out_o, *settled = bind((away_1, extra_1, out_o, *query_halves, *got_1st))
        query_halves, got_1st = settled[:4], settled[4:]
        kept_1 = (terms_1[:2].astype(F32) + away_1.astype(F32)).astype(BF)
        blocks_1, owns_1 = pairs_chip(terms_1, own_1, away_1, extra_1)
        out_1, blocks_1, chain_o.out = bind((kept_1[1], blocks_1, out_o))
        chain_o.move()
        got_1 = net.x(out_1)
        got_2 = net.deal(after(second, out_1))
        arrays = [turned_one, turned_other, *prompts, *query_halves, blocks_0, *owns_0, blocks_1, *owns_1]
        steps_query = [(m // 2, (m % 2) * rows, 6 + m, None) for m in range(4)]
        steps_pair = []
        for m in batches:
            steps_pair += [(2 + j, m * block, 10 + 3 * m, j) for j in range(4)]
            steps_pair += [(j, m * rows + block, 11 + 3 * m + j, None) for j in range(2)]
        query_terms = joint_terms(
            net.left_starts, arrays, [steps_query, steps_pair], [head_width // 2, pair_width], size
        )
        got_1, *query_terms = bind((got_1, *query_terms))
        chain_q = Chain(net, *query_terms)
        (query_0,) = advance([chain_q], query_0)
        grad_pairs = [
            pair_grads(kept[0].astype(F32) + got.astype(F32), own)
            for kept, got, own in ((kept_0, got_0, own_0), (kept_1, after(got_1, query_0), own_1))
        ]
        source_0 = finish_of(0, dmid_0, query_0, grad_pairs[0])
        source_0, third = bind((source_0, third))
        source_1 = finish_of(1, dmid_1, after(grad_query[1], source_0), grad_pairs[1])
        source_0, source_1, *got_2 = settle([chain_q, chain_o], source_0, source_1, *got_2)
        (theirs,) = advance([chain_q], theirs)
        chain_o.got = after(chain_o.got, theirs)
        (theirs,) = advance([chain_o], theirs)
        layer_out = output(hids, downs, [theirs], middle, 0, rows)
        (layer_out,) = settle([chain_q, chain_o], layer_out)
        (held_q,) = bind((chain_q.ready(),))
        held_q, first, second, third = bind((held_q, first, second, third))
        chain_o.got = after(chain_o.got, held_q)
        held_q = net.z_sum(held_q)
        chain_o.ready()
        chain_o.move()
        got_3 = net.deal(third)
        mine_1, theirs_1 = net.dealt(first, got_1st)
        mine_2, theirs_2 = net.dealt(second, got_2)
        mine_3, theirs_3 = net.dealt(third, got_3)
        gate_grad, up_grad, down_grad, sums = widen(
            net.c[None].astype(jnp.int32),
            [mine_1, mine_2, mine_3],
            [theirs_1, theirs_2, theirs_3],
            gate_weight,
            up_weight,
        )
        held_q, sums = settle([chain_o], held_q, sums)
        got_q = net.deal(held_q)
        held_o = chain_o.total()
        got_o = net.deal(held_o)
        output_rows = [value[0] for value in net.dealt(held_o, got_o)]
        query_rows = [value[0] for value in net.dealt(held_q, got_q)]
        pair_rows = [value[:, head_width // 2 :] for value in query_rows]
        query_rows = [value[:, : head_width // 2] for value in query_rows]

        def columns_of(rows_of):
            mine, theirs = (value.astype(F32) for value in rows_of)
            return jnp.where(net.c == 0, mine, theirs), jnp.where(net.c == 0, theirs, mine)

        output_grad = jnp.concatenate(columns_of(output_rows), axis=1)
        query_grad = jnp.concatenate(columns_of(query_rows), axis=1)
        key_grad, value_grad = columns_of(pair_rows)
        down_grad = down_grad.T
        feed_gain_grad = sums[:, 0] / feed_gain.astype(F32)
        grad_source = [source_0, source_1]
    else:
        grad_query, grad_pairs, dmids = [], [], []
        for m in batches:
            dmid, grad_mixed = unmerge(middle[m], upstream, m, gain_two, output_full, backs[m])
            query_m, terms, own = back_of(m, grad_mixed, 0, KV_HEADS)
            dmids.append(dmid)
            grad_query.append(query_m)
            grad_pairs.append(pair_grads(net.sum_pairs(terms), own))
        lefts_one = [(turned_one, m) for m in batches]
        lefts_mixed = [(value, 0) for value in mixed]
        terms = [
            grad_terms(net.left_starts, lefts_mixed, dmids, False, size, 640),
            grad_terms(net.left_starts, lefts_one, grad_query, True, size, 640),
            grad_terms(net.left_starts, lefts_one, grad_pairs, True, size, 640),
        ]
        output_grad, query_grad, pair_grad = [net.whole_sum(term[0], 0) for term in terms]
        key_grad, value_grad = pair_grad[:, :pair_width], pair_grad[:, pair_width:]
        feed_grads = net.whole_sum(feed_terms[0][0].reshape(3, width, hidden_width), 1)
        gate_grad, up_grad, down_grad = feed_grads[0], feed_grads[1], feed_grads[2].T
        layer_out = output(hids, downs, [], middle, 0, rows)
        grad_source = [finish_of(m, dmids[m], grad_query[m], grad_pairs[m]) for m in batches]

    def gain_grad(gain, *both):
        terms = sum(jnp.sum(weight.astype(F32) * grad, axis=1) for weight, grad in both)
        return terms / gain.astype(F32)

    attention_gain_grad = gain_grad(
        attention_gain, (query_weight, query_grad), (key_weight, key_grad), (value_weight, value_grad)
    )
    if not fast:
        feed_gain_grad = gain_grad(feed_gain, (gate_weight, gate_grad), (up_weight, up_grad))
    return (
        layer_out.reshape(tokens.shape),
        jnp.stack(grad_source),
        query_grad,
        key_grad,
        value_grad,
        output_grad,
        attention_gain_grad,
        gate_grad,
        up_grad,
        down_grad,
        feed_gain_grad,
    )


def solution(mesh):
    return jax.shard_map(
        on_device,
        mesh=mesh,
        in_specs=(
            P(None, ("rep", "shard"), None),
            P(None, ("rep", "shard"), None),
            P(None, "rep", None),
            P("shard", None),
            P("shard", None),
            P("shard", None),
            P("shard", None),
            P("shard"),
            P("shard", None),
            P("shard", None),
            P(None, "shard"),
            P("shard"),
        ),
        out_specs=(
            P(None, ("rep", "shard"), None),
            P(None, ("rep", "shard"), None),
            P("shard", None),
            P("shard", None),
            P("shard", None),
            P("shard", None),
            P("shard"),
            P("shard", None),
            P("shard", None),
            P(None, "shard"),
            P("shard"),
        ),
        check_vma=False,
    )
```

profile of v0, /device:TPU:1, one launch (start us, length us, event | category | flops | bytes accessed | tf_op | source)
XLA Modules:
  0.0 659.0 jit_solution(1673076987533589226)
XLA Ops:
  20.4 4.6 prepare.1.refs_1_
  29.3 5.4 project.2
  36.7 9.4 %collective-permute-done.7.refs_5_ = bf16[320,1280]{1,0:T(8,128)(2,1)} collective-permute-done((bf16[320,1280]{1,0:T(8,128)(2,1)}, bf16[320,1280]{1,0:T(8,128)(2,1)}, u32[]{:S(2)}, u32[]{:S(2)}) %collective-permute-start.7) | collective-permute-done | bytes 819232 | tf_op jit(solution)/shard_map/ppermute | solution.py:630
  51.7 6.1 collective-permute-done.6.refs_3_.refs_7_.refs_10_.refs_14_
  61.2 7.8 %project.3 = (bf16[1280,1024]{1,0:T(8,128)(2,1)}, bf16[1280,1280]{1,0:T(8,128)(2,1)}) custom-call(s32[4]{0:T(128)} %pad_add_fusion.2.refs_0_, bf16[1280,1024]{1,0:T(8,128)(2,1)} %prepare.1.refs_1_, f32[32,1024]{1,0:T(8,128)} %get-tuple-element.474.refs_2_.refs_1_, f32[32,1024]{1,0:T(8,128)} %get-tuple-element.473.refs_3_.refs_2_, bf16[320,1280]{1,0:T(8,128)(2,1)} %refs_4_.2, ...), custom_call_target="tpu_custom_call" | custom-call | flops 3355443200 | bytes 9830400 | tf_op jit(solution)/shard_map/project/pallas_call | solution.py:212
  69.1 30.8 %attend.2 = (bf16[1280,512]{1,0:T(8,128)(2,1)}, f32[5,4,512]{2,1,0:T(4,128)}) custom-call(s32[2,4]{1,0:T(2,128)} %subtract_multiply_fusion.refs_0_, bf16[1280,1024]{1,0:T(8,128)(2,1)} %get-tuple-element.211.refs_1_.refs_5_, bf16[640,256]{1,0:T(8,128)(2,1)} %get-tuple-element.456.refs_2_.refs_6_.refs_9_.refs_13_, ...), custom_call_target="tpu_custom_call" | custom-call | flops 30000001024 | bytes 5000000 | tf_op jit(solution)/shard_map/attend/pallas_call | solution.py:56
  117.4 30.6 %attend.3 = (bf16[1280,512]{1,0:T(8,128)(2,1)}, f32[5,4,512]{2,1,0:T(4,128)}) custom-call(s32[2,4]{1,0:T(2,128)} %subtract_multiply_fusion.refs_0_, bf16[1280,1024]{1,0:T(8,128)(2,1)} %get-tuple-element.211.refs_1_.refs_5_, bf16[640,256]{1,0:T(8,128)(2,1)} %get-tuple-element.455.refs_2_.refs_6_.refs_9_.refs_13_, ...), custom_call_target="tpu_custom_call" | custom-call | flops 30000001024 | bytes 5000000 | tf_op jit(solution)/shard_map/attend/pallas_call | solution.py:56
  149.9 5.3 collective-permute-done.22.refs_6_
  157.4 7.9 %merge.2 = (f32[512,1280]{1,0:T(8,128)}, bf16[512,1280]{1,0:T(8,128)(2,1)}, bf16[1280,1280]{1,0:T(8,128)(2,1)}) custom-call(s32[4]{0:T(128)} %pad_add_fusion.2.refs_0_, bf16[1280,512]{1,0:T(8,128)(2,1)} %get-tuple-element.224.refs_1_.refs_6_, bf16[1024,1280]{1,0:T(8,128)(2,1)} %bitcast.221, f32[1,1280]{1,0:T(1,128)} %get-tuple-element.471.refs_3_.gain_ref, ...), custom_call_target="tpu_custom_call" | custom-call | flops 1677721600 | bytes 16000000 | tf_op jit(solution)/shard_map/merge/pallas_call | solution.py:368
  165.4 6.7 %merge.3 = (f32[512,1280]{1,0:T(8,128)}, bf16[512,1280]{1,0:T(8,128)(2,1)}) custom-call(s32[4]{0:T(128)} %pad_add_fusion.2.refs_0_, bf16[1280,512]{1,0:T(8,128)(2,1)} %get-tuple-element.223.refs_1_.refs_6_.refs_2_, bf16[1024,1280]{1,0:T(8,128)(2,1)} %bitcast.222, f32[1,1280]{1,0:T(1,128)} %get-tuple-element.471.refs_3_.gain_ref, ...), custom_call_target="tpu_custom_call" | custom-call | flops 1677721600 | bytes 16000000 | tf_op jit(solution)/shard_map/merge/pallas_call | solution.py:368
  178.1 35.2 %feed.3 = (bf16[3,640,512]{2,1,0:T(8,128)(2,1)}, bf16[3,640,512]{2,1,0:T(8,128)(2,1)}, bf16[512,1280]{1,0:T(8,128)(2,1)}, bf16[512,1280]{1,0:T(8,128)(2,1)}, bf1...) custom-call(s32[2]{0:T(128)} %pad_add_fusion.1.refs_0_.refs_1_, ...), custom_call_target="tpu_custom_call" | custom-call | flops 21474836480 | bytes 40632320 | tf_op jit(solution)/shard_map/feed/pallas_call | solution.py:298
  213.6 4.3 all-gather.6.cloned.1.call-done
  217.9 46.8 %feed.4 = (bf16[2,640,768]{2,1,0:T(8,128)(2,1)}, bf16[1,640,768]{2,1,0:T(8,128)(2,1)}, bf16[2,640,768]{2,1,0:T(8,128)(2,1)}, bf16[1,640,768]{2,1,0:T(8,128)(2,1)...) custom-call(s32[2]{0:T(128)} %pad_add_fusion.1.refs_0_.refs_1_, ...), custom_call_target="tpu_custom_call" | custom-call | flops 32212254720 | bytes 45219840 | tf_op jit(solution)/shard_map/feed/pallas_call | solution.py:298
  268.7 35.0 %feed.5 = (bf16[3,640,512]{2,1,0:T(8,128)(2,1)}, bf16[3,640,512]{2,1,0:T(8,128)(2,1)}, bf16[512,1280]{1,0:T(8,128)(2,1)}, bf16[512,1280]{1,0:T(8,128)(2,1)}, bf1...) custom-call(s32[2]{0:T(128)} %pad_add_fusion.1.refs_0_.refs_1_, ...), custom_call_target="tpu_custom_call" | custom-call | flops 21474836480 | bytes 40632320 | tf_op jit(solution)/shard_map/feed/pallas_call | solution.py:298
  303.7 6.3 collective-permute-done.30
  324.3 9.0 %unmerge.2 = (bf16[512,1280]{1,0:T(8,128)(2,1)}, bf16[1280,512]{1,0:T(8,128)(2,1)}) custom-call(f32[512,1280]{1,0:T(8,128)} %get-tuple-element.261.mid_ref.refs_7_, bf16[1024,1280]{1,0:T(8,128)(2,1)} %bitcast.232, f32[1,1280]{1,0:T(1,128)} %get-tuple-element.471.refs_3_.gain_ref, bf16[1280,1280]{1,0:T(8,128)(2,1)} %get-tuple-element.227.refs_4_.whole_ref, ...), custom_call_target="tpu_custom_call" | custom-call | flops 1677721600 | bytes 16000000 | tf_op jit(solution)/shard_map/unmerge/pallas_call | solution.py:407
  333.4 9.4 %output.2 = bf16[1024,1280]{1,0:T(8,128)(2,1)} custom-call(bf16[2048,512]{1,0:T(8,128)(2,1)} %get-tuple-element.231.refs_0_, bf16[2048,768]{1,0:T(8,128)(2,1)} %get-tuple-element.240.refs_1_, bf16[2048,512]{1,0:T(8,128)(2,1)} %get-tuple-element.268.refs_2_, bf16[1280,512]{1,0:T(8,128)(2,1)} %get-tuple-element.269.refs_3_, ...), custom_call_target="tpu_custom_call" | custom-call | flops 5000000000 | bytes 16000000 | tf_op jit(solution)/shard_map/output/pallas_call | solution.py:513
  348.7 34.8 %attend_back.3 = (bf16[1280,512]{1,0:T(8,128)(2,1)}, bf16[4,2,5,64,256]{4,3,2,1,0:T(8,128)(2,1)}, bf16[2,5,64,256]{3,2,1,0:T(8,128)(2,1)}) custom-call(s32[2,4]{1,0:T(2,128)} %subtract_multiply_fusion.refs_0_, f32[32,1024]{1,0:T(8,128)} %get-tuple-element.474.refs_2_.refs_1_, f32[32,1024]{1,0:T(8,128)} %get-tuple-element.473.refs_3_.refs_2_, ...), custom_call_target="tpu_custom_call" | custom-call | flops 40000000000 | bytes 5000000 | tf_op jit(solution)/shard_map/attend_back/pallas_call | solution.py:146
  397.7 9.3 %unmerge.3 = (bf16[512,1280]{1,0:T(8,128)(2,1)}, bf16[1280,512]{1,0:T(8,128)(2,1)}) custom-call(f32[512,1280]{1,0:T(8,128)} %get-tuple-element.290.mid_ref.refs_8_, bf16[1024,1280]{1,0:T(8,128)(2,1)} %bitcast.233, f32[1,1280]{1,0:T(1,128)} %get-tuple-element.471.refs_3_.gain_ref, bf16[1280,1280]{1,0:T(8,128)(2,1)} %get-tuple-element.227.refs_4_.whole_ref, ...), custom_call_target="tpu_custom_call" | custom-call | flops 1677721600 | bytes 16000000 | tf_op jit(solution)/shard_map/unmerge/pallas_call | solution.py:407
  415.8 22.2 %attend_back.4 = (bf16[768,512]{1,0:T(8,128)(2,1)}, bf16[4,2,3,64,256]{4,3,2,1,0:T(8,128)(2,1)}, bf16[2,3,64,256]{3,2,1,0:T(8,128)(2,1)}) custom-call(s32[2,4]{1,0:T(2,128)} %subtract_multiply_fusion.refs_0_, f32[32,1024]{1,0:T(8,128)} %get-tuple-element.474.refs_2_.refs_1_, f32[32,1024]{1,0:T(8,128)} %get-tuple-element.473.refs_3_.refs_2_, ...), custom_call_target="tpu_custom_call" | custom-call | flops 24000000000 | bytes 3000000 | tf_op jit(solution)/shard_map/attend_back/pallas_call | solution.py:146
  442.5 8.7 %grad_terms.1 = (bf16[640,640]{1,0:T(8,128)(2,1)}, bf16[640,640]{1,0:T(8,128)(2,1)}) custom-call(s32[2]{0:T(128)} %pad_add_fusion.1.refs_0_.refs_1_, bf16[1280,512]{1,0:T(8,128)(2,1)} %get-tuple-element.224.refs_1_.refs_6_, bf16[1280,512]{1,0:T(8,128)(2,1)} %get-tuple-element.223.refs_1_.refs_6_.refs_2_, bf16[1280,512]{1,0:T(8,128)(2,1)} %collective-permute-done.46.refs_3_, ...), custom_call_target="tpu_custom_call" | custom-call | flops 3355443200 | bytes 8000000 | tf_op jit(solution)/shard_map/grad_terms/pallas_call | solution.py:450
  458.2 15.2 %attend_back.5 = (bf16[512,512]{1,0:T(8,128)(2,1)}, bf16[4,2,2,64,256]{4,3,2,1,0:T(8,128)(2,1)}, bf16[2,2,64,256]{3,2,1,0:T(8,128)(2,1)}) custom-call(s32[2,4]{1,0:T(2,128)} %subtract_multiply_fusion.refs_0_, f32[32,1024]{1,0:T(8,128)} %get-tuple-element.474.refs_2_.refs_1_, f32[32,1024]{1,0:T(8,128)} %get-tuple-element.473.refs_3_.refs_2_, ...), custom_call_target="tpu_custom_call" | custom-call | flops 16000000000 | bytes 2000000 | tf_op jit(solution)/shard_map/attend_back/pallas_call | solution.py:146
  494.9 15.0 %joint_terms.1 = (bf16[640,960]{1,0:T(8,128)(2,1)}, bf16[640,960]{1,0:T(8,128)(2,1)}) custom-call(s32[2]{0:T(128)} %pad_add_fusion.1.refs_0_.refs_1_, bf16[1280,1024]{1,0:T(8,128)(2,1)} %prepare.1.refs_1_, bf16[1280,1024]{1,0:T(8,128)(2,1)} %collective-permute-done.58.refs_2_, bf16[1280,512]{1,0:T(8,128)(2,1)} %pad_maximum_fusion.9.refs_3_, ...), custom_call_target="tpu_custom_call" | custom-call | flops 6000000000 | bytes 14000000 | tf_op jit(solution)/shard_map/joint_terms/pallas_call | solution.py:481
  515.2 8.6 %finish.2 = bf16[512,1280]{1,0:T(8,128)(2,1)} custom-call(bf16[1024,1280]{1,0:T(8,128)(2,1)} %bitcast.223, f32[1,1280]{1,0:T(1,128)} %get-tuple-element.472.gain_ref, bf16[512,1280]{1,0:T(8,128)(2,1)} %get-tuple-element.299.dmid_ref, bf16[1280,512]{1,0:T(8,128)(2,1)} %get-tuple-element.360.dq_ref, bf16[640,512]{1,0:T(8,128)(2,1)} %bitcast.240, ...), custom_call_target="tpu_custom_call" | custom-call | flops 2516582400 | bytes 12000000 | tf_op jit(solution)/shard_map/finish/pallas_call | solution.py:541
  523.8 11.7 %all-reduce.9.cloned.1.call-done = bf16[3,320,512]{2,1,0:T(8,128)(2,1)} async-done(((bf16[3,320,512]{2,1,0:T(8,128)(2,1)}), bf16[3,320,512]{2,1,0:T(8,128)(2,1)}) %all-reduce.9.cloned.1.call-update) | async-done | bytes 983056 | tf_op jit(solution)/shard_map/psum | solution.py:706
  536.4 8.4 %finish.3 = bf16[512,1280]{1,0:T(8,128)(2,1)} custom-call(bf16[1024,1280]{1,0:T(8,128)(2,1)} %bitcast.224, f32[1,1280]{1,0:T(1,128)} %get-tuple-element.472.gain_ref, bf16[512,1280]{1,0:T(8,128)(2,1)} %get-tuple-element.300.dmid_ref, bf16[1280,512]{1,0:T(8,128)(2,1)} %copy-done.1, bf16[640,512]{1,0:T(8,128)(2,1)} %bitcast.241, ...), custom_call_target="tpu_custom_call" | custom-call | flops 2516582400 | bytes 12000000 | tf_op jit(solution)/shard_map/finish/pallas_call | solution.py:541
  550.8 11.7 %output.3 = bf16[1024,1280]{1,0:T(8,128)(2,1)} custom-call(bf16[2048,512]{1,0:T(8,128)(2,1)} %get-tuple-element.231.refs_0_, bf16[2048,768]{1,0:T(8,128)(2,1)} %get-tuple-element.240.refs_1_, bf16[2048,512]{1,0:T(8,128)(2,1)} %get-tuple-element.268.refs_2_, bf16[1280,512]{1,0:T(8,128)(2,1)} %get-tuple-element.269.refs_3_, ...), custom_call_target="tpu_custom_call" | custom-call | flops 5000000000 | bytes 16000000 | tf_op jit(solution)/shard_map/output/pallas_call | solution.py:513
  579.7 6.7 %collective-permute-done.68 = bf16[3,320,512]{2,1,0:T(8,128)(2,1)S(1)} collective-permute-done((bf16[3,320,512]{2,1,0:T(8,128)(2,1)S(1)}, bf16[3,320,512]{2,1,0:T(8,128)(2,1)S(1)}, u32[]{:S(2)}, u32[]{:S(2)}) %collective-permute-start.68) | collective-permute-done | bytes 983072 | tf_op jit(solution)/shard_map/ppermute | solution.py:719
  586.4 4.5 collective-permute-done.69
  593.6 14.9 %widen.1 = (f32[320,3584]{1,0:T(8,128)}, f32[320,3584]{1,0:T(8,128)}, f32[320,3584]{1,0:T(8,128)}, f32[320,1]{1,0:T(8,128)}) custom-call(s32[1]{0:T(128)} %bitcast.103.refs_0_, bf16[3,320,512]{2,1,0:T(8,128)(2,1)} %get-tuple-element.462.refs_1_, bf16[3,320,768]{2,1,0:T(8,128)(2,1)} %get-tuple-element.438.refs_2_, ...), custom_call_target="tpu_custom_call" | custom-call | bytes 26000000 | tf_op jit(solution)/shard_map/widen/pallas_call | solution.py:609
  608.5 12.3 %all-reduce.11.cloned.1.call-done = bf16[1,320,960]{2,1,0:T(8,128)(2,1)} async-done(((bf16[1,320,960]{2,1,0:T(8,128)(2,1)}), bf16[1,320,960]{2,1,0:T(8,128)(2,1)}) %all-reduce.11.cloned.1.call-update) | async-done | bytes 614416 | tf_op jit(solution)/shard_map/psum | solution.py:706
  637.5 7.8 %collective-permute-done.70 = bf16[1,320,960]{2,1,0:T(8,128)(2,1)S(1)} collective-permute-done((bf16[1,320,960]{2,1,0:T(8,128)(2,1)S(1)}, bf16[1,320,960]{2,1,0:T(8,128)(2,1)S(1)}, u32[]{:S(2)}, u32[]{:S(2)}) %collective-permute-start.70) | collective-permute-done | bytes 614432 | tf_op jit(solution)/shard_map/ppermute | solution.py:719
  (374 shorter events, 191.1 us)
Async XLA Ops:
  7.2 169.9 %all-gather.4.cloned.1.call-start = ((), (), s32[]{:S(2)}) async-start(), calls=%async_computation | async-start | bytes 2211840 | tf_op jit(solution)/shard_map/all_gather | solution.py:702
  13.7 46.0 %collective-permute-start.8 = (bf16[320,1280]{1,0:T(8,128)(2,1)}, bf16[320,1280]{1,0:T(8,128)(2,1)}, u32[]{:S(2)}, u32[]{:S(2)}) collective-permute-start(bf16[320,1280]{1,0:T(8,128)(2,1)} %refs_4_.2), channel_id=1, source_target_pairs={{0,1},{1,0},{2,3},{3,2},{4,5},{5,4},{6,7},{7,6},{8,9},{9,8},{10,11... | collective-permute-start | bytes 2457608 | tf_op jit(solution)/shard_map/ppermute | solution.py:630
  19.3 30.6 %collective-permute-start.14 = (bf16[3,320,512]{2,1,0:T(8,128)(2,1)S(1)}, bf16[3,320,512]{2,1,0:T(8,128)(2,1)}, u32[]{:S(2)}, u32[]{:S(2)}) collective-permute-start(bf16[3,320,512]{2,1,0:T(8,128)(2,1)S(1)} %pad_maximum_fusion.12), channel_id=1, source_target_pairs={{0,1},{1,0},{2,3},{3,2},{4,5},{5,4},{6,7},{7,6},{8,9},{9,8},{10,11... | collective-permute-start | bytes 2949128 | tf_op jit(solution)/shard_map/ppermute | solution.py:630
  49.9 50.0 %collective-permute-start.13 = (bf16[640,256]{1,0:T(8,128)(2,1)}, bf16[640,256]{1,0:T(8,128)(2,1)}, u32[]{:S(2)}, u32[]{:S(2)}) collective-permute-start(bf16[640,256]{1,0:T(8,128)(2,1)} %get-tuple-element.455.refs_2_.refs_6_.refs_9_.refs_13_), channel_id=1, source_target_pairs={{0,2},{1,3},{2,0},{3,1},{4,6},{5,7},{6,4},{7,5},{8,10},{9,11},{10,... | collective-permute-start | bytes 983048 | tf_op jit(solution)/shard_map/ppermute | solution.py:630
  59.7 40.2 %collective-permute-start.12 = (bf16[320,1280]{1,0:T(8,128)(2,1)}, bf16[320,1280]{1,0:T(8,128)(2,1)}, u32[]{:S(2)}, u32[]{:S(2)}) collective-permute-start(bf16[320,1280]{1,0:T(8,128)(2,1)} %refs_4_.3), channel_id=1, source_target_pairs={{0,2},{1,3},{2,0},{3,1},{4,6},{5,7},{6,4},{7,5},{8,10},{9,11},{10,... | collective-permute-start | bytes 2457608 | tf_op jit(solution)/shard_map/ppermute | solution.py:630
  61.1 38.7 %collective-permute-start.15 = (bf16[240,512]{1,0:T(8,128)(2,1)}, bf16[240,512]{1,0:T(8,128)(2,1)}, u32[]{:S(2)}, u32[]{:S(2)}) collective-permute-start(bf16[240,512]{1,0:T(8,128)(2,1)} %constant_dynamic-slice_fusion.18), channel_id=1, source_target_pairs={{0,2},{1,3},{2,0},{3,1},{4,6},{5,7},{6,4},{7,5},{8,10},{9,11},{10,... | collective-permute-start | bytes 737288 | tf_op jit(solution)/shard_map/ppermute | solution.py:630
  109.8 108.1 %all-gather.6.cloned.1.call-start = ((), (), s32[]{:S(2)}) async-start(), calls=%async_computation.1 | async-start | bytes 3317760 | tf_op jit(solution)/shard_map/all_gather | solution.py:702
  113.0 35.0 %collective-permute-start.21 = (bf16[240,512]{1,0:T(8,128)(2,1)}, bf16[240,512]{1,0:T(8,128)(2,1)}, u32[]{:S(2)}, u32[]{:S(2)}) collective-permute-start(bf16[240,512]{1,0:T(8,128)(2,1)} %constant_dynamic-slice_fusion.16), channel_id=1, source_target_pairs={{0,2},{1,3},{2,0},{3,1},{4,6},{5,7},{6,4},{7,5},{8,10},{9,11},{10,... | collective-permute-start | bytes 737288 | tf_op jit(solution)/shard_map/ppermute | solution.py:630
  116.7 31.4 %collective-permute-start.19 = (bf16[240,768]{1,0:T(8,128)(2,1)S(1)}, bf16[240,768]{1,0:T(8,128)(2,1)S(1)}, u32[]{:S(2)}, u32[]{:S(2)}) collective-permute-start(bf16[240,768]{1,0:T(8,128)(2,1)S(1)} %constant_dynamic-slice_fusion.17), channel_id=1, source_target_pairs={{0,2},{1,3},{2,0},{3,1},{4,6},{5,7},{6,4},{7,5},{8,10},{9,11},{10,... | collective-permute-start | bytes 1105928 | tf_op jit(solution)/shard_map/ppermute | solution.py:630
  148.8 119.8 %all-gather.8.cloned.1.call-start = ((), (), s32[]{:S(2)}) async-start(), calls=%async_computation.2 | async-start | bytes 2211840 | tf_op jit(solution)/shard_map/all_gather | solution.py:702
  175.7 37.9 %collective-permute-start.27 = (bf16[1280,512]{1,0:T(8,128)(2,1)}, bf16[1280,512]{1,0:T(8,128)(2,1)}, u32[]{:S(2)}, u32[]{:S(2)}) collective-permute-start(bf16[1280,512]{1,0:T(8,128)(2,1)} %pad_maximum_fusion.9.refs_3_), channel_id=1, source_target_pairs={{0,2},{1,3},{2,0},{3,1},{4,6},{5,7},{6,4},{7,5},{8,10},{9,11},{10,... | collective-permute-start | bytes 3932168 | tf_op jit(solution)/shard_map/ppermute | solution.py:630
  177.0 210.6 %all-reduce.5.cloned.1.call-start = ((), (), s32[]{:S(2)}) async-start(), calls=%async_computation.3 | async-start | bytes 1966080 | tf_op jit(solution)/shard_map/psum | solution.py:706
  213.3 51.4 %collective-permute-start.28 = (bf16[1920,512]{1,0:T(8,128)(2,1)}, bf16[1920,512]{1,0:T(8,128)(2,1)}, u32[]{:S(2)}, u32[]{:S(2)}) collective-permute-start(bf16[1920,512]{1,0:T(8,128)(2,1)} %bitcast.281), channel_id=1, source_target_pairs={{0,2},{1,3},{2,0},{3,1},{4,6},{5,7},{6,4},{7,5},{8,10},{9,11},{10,... | collective-permute-start | bytes 5898248 | tf_op jit(solution)/shard_map/ppermute | solution.py:630
  267.2 36.5 %collective-permute-start.29 = (bf16[3,320,512]{2,1,0:T(8,128)(2,1)}, bf16[3,320,512]{2,1,0:T(8,128)(2,1)}, u32[]{:S(2)}, u32[]{:S(2)}) collective-permute-start(bf16[3,320,512]{2,1,0:T(8,128)(2,1)} %fusion.6), channel_id=1, source_target_pairs={{0,4},{4,0},{8,12},{12,8},{16,20},{20,16},{24,28},{28,24},{1,5},{5... | collective-permute-start | bytes 2949128 | tf_op jit(solution)/shard_map/ppermute | solution.py:630
  267.4 42.6 %collective-permute-start.30 = (bf16[1280,768]{1,0:T(8,128)(2,1)}, bf16[1280,768]{1,0:T(8,128)(2,1)}, u32[]{:S(2)}, u32[]{:S(2)}) collective-permute-start(bf16[1280,768]{1,0:T(8,128)(2,1)} %bitcast.57), channel_id=1, source_target_pairs={{0,2},{1,3},{2,0},{3,1},{4,6},{5,7},{6,4},{7,5},{8,10},{9,11},{10,... | collective-permute-start | bytes 5898248 | tf_op jit(solution)/shard_map/ppermute | solution.py:630
  323.6 71.6 %collective-permute-start.39 = (bf16[512,1280]{1,0:T(8,128)(2,1)}, bf16[512,1280]{1,0:T(8,128)(2,1)}, u32[]{:S(2)}, u32[]{:S(2)}) collective-permute-start(bf16[512,1280]{1,0:T(8,128)(2,1)} %get-tuple-element.292), channel_id=1, source_target_pairs={{0,1},{1,0},{2,3},{3,2},{4,5},{5,4},{6,7},{7,6},{8,9},{9,8},{10,11... | collective-permute-start | bytes 3932168 | tf_op jit(solution)/shard_map/ppermute | solution.py:630
  324.3 72.9 %collective-permute-start.40 = (bf16[512,1280]{1,0:T(8,128)(2,1)}, bf16[512,1280]{1,0:T(8,128)(2,1)}, u32[]{:S(2)}, u32[]{:S(2)}) collective-permute-start(bf16[512,1280]{1,0:T(8,128)(2,1)} %get-tuple-element.294), channel_id=1, source_target_pairs={{0,1},{1,0},{2,3},{3,2},{4,5},{5,4},{6,7},{7,6},{8,9},{9,8},{10,11... | collective-permute-start | bytes 3932168 | tf_op jit(solution)/shard_map/ppermute | solution.py:630
  333.3 143.1 %all-reduce.7.cloned.1.call-start = ((), (), s32[]{:S(2)}) async-start(), calls=%async_computation.4 | async-start | bytes 2949120 | tf_op jit(solution)/shard_map/psum | solution.py:706
  345.8 41.4 %collective-permute-start.36 = (bf16[1,320,768]{2,1,0:T(8,128)(2,1)}, bf16[1,320,768]{2,1,0:T(8,128)(2,1)}, u32[]{:S(2)}, u32[]{:S(2)}) collective-permute-start(bf16[1,320,768]{2,1,0:T(8,128)(2,1)} %fusion.16), channel_id=1, source_target_pairs={{0,4},{4,0},{8,12},{12,8},{16,20},{20,16},{24,28},{28,24},{1,5},{5... | collective-permute-start | bytes 1474568 | tf_op jit(solution)/shard_map/ppermute | solution.py:630
  346.1 41.4 %collective-permute-start.37 = (bf16[1024,1280]{1,0:T(8,128)(2,1)}, bf16[1024,1280]{1,0:T(8,128)(2,1)}, u32[]{:S(2)}, u32[]{:S(2)}) collective-permute-start(bf16[1024,1280]{1,0:T(8,128)(2,1)} %output.2), channel_id=1, source_target_pairs={{0,1},{1,0},{2,3},{3,2},{4,5},{5,4},{6,7},{7,6},{8,9},{9,8},{10,11... | collective-permute-start | bytes 7864328 | tf_op jit(solution)/shard_map/ppermute | solution.py:630
  347.5 62.0 %collective-permute-start.38 = (bf16[1920,512]{1,0:T(8,128)(2,1)}, bf16[1920,512]{1,0:T(8,128)(2,1)}, u32[]{:S(2)}, u32[]{:S(2)}) collective-permute-start(bf16[1920,512]{1,0:T(8,128)(2,1)} %bitcast.278), channel_id=1, source_target_pairs={{0,2},{1,3},{2,0},{3,1},{4,6},{5,7},{6,4},{7,5},{8,10},{9,11},{10,... | collective-permute-start | bytes 5898248 | tf_op jit(solution)/shard_map/ppermute | solution.py:630
  392.1 143.4 %all-reduce.9.cloned.1.call-start = ((), (), s32[]{:S(2)}) async-start(), calls=%async_computation.5 | async-start | bytes 1966080 | tf_op jit(solution)/shard_map/psum | solution.py:706
  397.2 45.3 %collective-permute-start.46 = (bf16[1280,512]{1,0:T(8,128)(2,1)}, bf16[1280,512]{1,0:T(8,128)(2,1)}, u32[]{:S(2)}, u32[]{:S(2)}) collective-permute-start(bf16[1280,512]{1,0:T(8,128)(2,1)} %get-tuple-element.224.refs_1_.refs_6_), channel_id=1, source_target_pairs={{0,1},{1,0},{2,3},{3,2},{4,5},{5,4},{6,7},{7,6},{8,9},{9,8},{10,11... | collective-permute-start | bytes 3932168 | tf_op jit(solution)/shard_map/ppermute | solution.py:630
  397.3 45.2 %collective-permute-start.47 = (bf16[1280,512]{1,0:T(8,128)(2,1)}, bf16[1280,512]{1,0:T(8,128)(2,1)}, u32[]{:S(2)}, u32[]{:S(2)}) collective-permute-start(bf16[1280,512]{1,0:T(8,128)(2,1)} %get-tuple-element.223.refs_1_.refs_6_.refs_2_), channel_id=1, source_target_pairs={{0,1},{1,0},{2,3},{3,2},{4,5},{5,4},{6,7},{7,6},{8,9},{9,8},{10,11... | collective-permute-start | bytes 3932168 | tf_op jit(solution)/shard_map/ppermute | solution.py:630
  414.0 37.1 %collective-permute-start.44 = (bf16[3,320,512]{2,1,0:T(8,128)(2,1)S(1)}, bf16[3,320,512]{2,1,0:T(8,128)(2,1)}, u32[]{:S(2)}, u32[]{:S(2)}) collective-permute-start(bf16[3,320,512]{2,1,0:T(8,128)(2,1)S(1)} %fusion.8), channel_id=1, source_target_pairs={{0,4},{4,0},{8,12},{12,8},{16,20},{20,16},{24,28},{28,24},{1,5},{5... | collective-permute-start | bytes 2949128 | tf_op jit(solution)/shard_map/ppermute | solution.py:630
  441.6 53.2 %collective-permute-start.58 = (bf16[1280,1024]{1,0:T(8,128)(2,1)}, bf16[1280,1024]{1,0:T(8,128)(2,1)}, u32[]{:S(2)}, u32[]{:S(2)}) collective-permute-start(bf16[1280,1024]{1,0:T(8,128)(2,1)} %prepare.1.refs_1_), channel_id=1, source_target_pairs={{0,1},{1,0},{2,3},{3,2},{4,5},{5,4},{6,7},{7,6},{8,9},{9,8},{10,11... | collective-permute-start | bytes 7864328 | tf_op jit(solution)/shard_map/ppermute | solution.py:630
  485.9 134.8 %all-reduce.11.cloned.1.call-start = ((), (), s32[]{:S(2)}) async-start(), calls=%async_computation.6 | async-start | bytes 1310720 | tf_op jit(solution)/shard_map/psum | solution.py:706
  492.0 52.8 %collective-permute-start.63 = (bf16[3,320,768]{2,1,0:T(8,128)(2,1)}, bf16[3,320,768]{2,1,0:T(8,128)(2,1)}, u32[]{:S(2)}, u32[]{:S(2)}) collective-permute-start(bf16[3,320,768]{2,1,0:T(8,128)(2,1)} %all-reduce.7.cloned.1.call-done), channel_id=1, source_target_pairs={{0,4},{1,0},{2,6},{3,2},{4,5},{5,1},{6,7},{7,3},{8,12},{9,8},{10,1... | collective-permute-start | bytes 4423688 | tf_op jit(solution)/shard_map/ppermute | solution.py:719
  492.7 52.2 %collective-permute-start.64 = (bf16[3,320,768]{2,1,0:T(8,128)(2,1)}, bf16[3,320,768]{2,1,0:T(8,128)(2,1)}, u32[]{:S(2)}, u32[]{:S(2)}) collective-permute-start(bf16[3,320,768]{2,1,0:T(8,128)(2,1)} %all-reduce.7.cloned.1.call-done), channel_id=1, source_target_pairs={{1,4},{3,6},{4,1},{6,3},{9,12},{11,14},{12,9},{14,11},{17,20},{19,... | collective-permute-start | bytes 4423688 | tf_op jit(solution)/shard_map/ppermute | solution.py:719
  513.3 31.6 %collective-permute-start.61 = (bf16[640,960]{0,1:T(8,128)(2,1)}, bf16[640,960]{0,1:T(8,128)(2,1)}, u32[]{:S(2)}, u32[]{:S(2)}) collective-permute-start(bf16[640,960]{0,1:T(8,128)(2,1)} %copy.90), channel_id=1, source_target_pairs={{0,2},{1,3},{2,0},{3,1},{4,6},{5,7},{6,4},{7,5},{8,10},{9,11},{10,... | collective-permute-start | bytes 3686408 | tf_op jit(solution)/shard_map/ppermute | solution.py:630
  514.8 30.0 %collective-permute-start.62 = (bf16[1,320,640]{2,1,0:T(8,128)(2,1)S(1)}, bf16[1,320,640]{2,1,0:T(8,128)(2,1)}, u32[]{:S(2)}, u32[]{:S(2)}) collective-permute-start(bf16[1,320,640]{2,1,0:T(8,128)(2,1)S(1)} %copy-done.31), channel_id=1, source_target_pairs={{0,4},{4,0},{8,12},{12,8},{16,20},{20,16},{24,28},{28,24},{1,5},{5... | collective-permute-start | bytes 1228808 | tf_op jit(solution)/shard_map/ppermute | solution.py:630
  571.8 36.7 %collective-permute-start.67 = (bf16[1,320,640]{2,1,0:T(8,128)(2,1)S(1)}, bf16[1,320,640]{2,1,0:T(8,128)(2,1)}, u32[]{:S(2)}, u32[]{:S(2)}) collective-permute-start(bf16[1,320,640]{2,1,0:T(8,128)(2,1)S(1)} %add_convert_fusion.8), channel_id=1, source_target_pairs={{0,16},{4,20},{8,24},{12,28},{16,0},{20,4},{24,8},{28,12},{1,17},{... | collective-permute-start | bytes 1228808 | tf_op jit(solution)/shard_map/ppermute | solution.py:630
  (97 other events, 994.9 us)
Sparse Core Ops, SparseCore 0:
  109.9 47.7 all-gather.3
  160.4 57.4 all-gather.5
  220.1 46.7 all-gather.7
  333.4 48.5 all-reduce.4
  392.2 64.2 all-reduce.6
  486.1 49.3 all-reduce.8
  570.8 49.9 all-reduce.10
where the time goes:
time: 670 us; the launch traced here: 659 us
  Pallas kernels  378 us (56%)
  waiting for transfers between devices  87.5 us (13%)
  other arithmetic  70.1 us (10%)
  starting transfers between devices  57.4 us (9%)
  local copies, waits for them, and re-layouts  50.5 us (8%)
  between operations  15.5 us (2%)
    pallas_call x3, Pallas kernels, feed(): pl.pallas_call(lambda *refs: feed_kernel(*refs, sets=sets, pieces=len(par...  117 us
    pallas_call x3, Pallas kernels, attend_back(): pl.pallas_call(lambda *refs: back_kernel(*refs, m=m, blocks=blocks), grid...  72.2 us
    pallas_call x2, Pallas kernels, attend(): pl.pallas_call(lambda *refs: attend_kernel(*refs, m=m, blocks=blocks), gr...  61.4 us
    ppermute x64, starting transfers between devices, partner(): return lax.ppermute(value, axis, [(i, i ^ bit) for i in range(size)])  41 us
    ppermute x64, waiting for transfers between devices, partner(): return lax.ppermute(value, axis, [(i, i ^ bit) for i in range(size)])  34.9 us
    ppermute x10, waiting for transfers between devices, deal(): lax.ppermute(held, ('rep', 'shard'), pairs)  24.2 us
    psum x4, waiting for transfers between devices, z_sum(): return lax.psum(value, 'rep', axis_index_groups=lines)  24 us
    pallas_call x2, Pallas kernels, output(): pl.pallas_call(lambda *refs: output_kernel(*refs, parts=len(hids), adds=l...  21.1 us
  transfers between devices with their start and end apart: 81, of which 19 were waited for; matrix products, arithmetic and copies ran while one was open for 14% of the time, Pallas kernels for 57%

commit v1 on v0

--- a/solution.py
+++ b/solution.py
@@ -175,7 +175,7 @@
         ],
         scratch_shapes=[pltpu.VMEM(((blocks + 1) * blk, GROUP * blk), BF)] * 2,
         compiler_params=pltpu.CompilerParams(vmem_limit_bytes=VMEM_BYTES),
-        cost_estimate=pl.CostEstimate(flops=8 * 10**9 * count, bytes_accessed=10**6 * count, transcendentals=0),
+        cost_estimate=pl.CostEstimate(flops=2 * 10**9 * count, bytes_accessed=10**6 * count, transcendentals=0),
         name="attend_back",
     )(gap, cosT, sinT, kcos, ksin, qT, aT, daT, lse, *pairs, *pairs, ownT, ownT)
 
@@ -900,7 +900,7 @@
         eighth_1, eighth_2 = [net.feed_eighth(part) for part in feed_cores[1:]]
         output_pieces = [output_weight, output_across, net.core(output_weight), net.core(output_across)]
         mixed_1, log_1 = attend(after(gap, mixed_0), query, pairs[1], own_pairs, micro, 1)
-        mixed_1, eighth_1, eighth_2 = bind((mixed_1, eighth_1, eighth_2))
+        mixed_1, eighth_1, eighth_2, *output_pieces[2:] = bind((mixed_1, eighth_1, eighth_2, *output_pieces[2:]))
         feed_parts += [net.feed_parts(feed_cores[1], eighth_1), net.feed_parts(feed_cores[2], eighth_2)]
         mixed, log_total = [mixed_0, mixed_1], [log_0, log_1]
         mixed_all = mixed + [net.core(value) for value in mixed]
@@ -1021,27 +1021,20 @@
         mixed_1, moved_0, moved_1, out_0 = advance([part_4], mixed_1, moved_0, moved_1, kept_0[1])
         got_0 = net.x(out_0)
         dmid_halves = [halves_0[0], halves_1[0], net.core(moved_0), net.core(moved_1)]
-        query_1, terms_1, own_1 = back_of(1, mixed_1, 0, 3)
-        output_terms = grad_terms(
-            net.left_starts, lefts_mixed, [after(value, query_1) for value in dmid_halves], False, size, 640
-        )
-
-        query_1, got_0, *output_terms = settle([part_4], query_1, got_0, *output_terms)
-        blocks_0, owns_0 = pairs_chip(terms_0, own_0, away_0, extra_0)
+        output_terms = grad_terms(net.left_starts, lefts_mixed, dmid_halves, False, size, 640)
         chain_o = Chain(net, *output_terms)
-        mixed_1, third, blocks_0 = advance([chain_o], after(mixed_1, query_1), part_4.total(), blocks_0)
-        third = net.z_sum(third, (1, 0))
+        (mixed_1,) = advance([chain_o], mixed_1)
         got_1st = net.deal(after(first, mixed_1))
-        query_1b, terms_1b, own_1b = back_of(1, mixed_1, 3, KV_HEADS)
-
-        query_1b, second = settle([chain_o], query_1b, second)
-        terms_1 = jnp.concatenate([terms_1, terms_1b], axis=2)
-        own_1 = jnp.concatenate([own_1, own_1b], axis=1)
-        grad_query = [query_0, jnp.concatenate([query_1, query_1b], axis=0)]
+        query_1, terms_1, own_1 = back_of(1, mixed_1, 0, KV_HEADS)
+
+        query_1, got_0, second = settle([part_4, chain_o], query_1, got_0, second)
+        grad_query = [query_0, query_1]
         halves = [split(value, 0) for value in grad_query]
         moved_0, moved_1, terms_1 = bind((halves[0][1], halves[1][1], terms_1))
         away_1, extra_1 = pairs_out(terms_1, own_1)
         query_halves = [halves[0][0], halves[1][0], net.core(moved_0), net.core(moved_1)]
+        blocks_0, owns_0 = pairs_chip(terms_0, own_0, away_0, extra_0)
+        third = net.z_sum(part_4.total(), (1, 0))
         (out_o,) = bind((chain_o.ready(),))
         away_1, extra_1, out_o, *settled = bind((away_1, extra_1, out_o, *query_halves, *got_1st))
         query_halves, got_1st = settled[:4], settled[4:]
@@ -1093,10 +1086,12 @@
             gate_weight,
             up_weight,
         )
-        held_q, sums = settle([chain_o], held_q, sums)
-        got_q = net.deal(held_q)
+        grad_source = jnp.stack([source_0, source_1])
+        sums, grad_source = settle([chain_o], sums, grad_source)
         held_o = chain_o.total()
         got_o = net.deal(held_o)
+        held_q, *got_o = bind((held_q, *got_o))
+        got_q = net.deal(held_q)
         output_rows = [value[0] for value in net.dealt(held_o, got_o)]
         query_rows = [value[0] for value in net.dealt(held_q, got_q)]
         pair_rows = [value[:, head_width // 2 :] for value in query_rows]
@@ -1111,7 +1106,6 @@
         key_grad, value_grad = columns_of(pair_rows)
         down_grad = down_grad.T
         feed_gain_grad = sums[:, 0] / feed_gain.astype(F32)
-        grad_source = [source_0, source_1]
     else:
         grad_query, grad_pairs, dmids = [], [], []
         for m in batches:
@@ -1132,7 +1126,7 @@
         feed_grads = net.whole_sum(feed_terms[0][0].reshape(3, width, hidden_width), 1)
         gate_grad, up_grad, down_grad = feed_grads[0], feed_grads[1], feed_grads[2].T
         layer_out = output(hids, downs, [], middle, 0, rows)
-        grad_source = [finish_of(m, dmids[m], grad_query[m], grad_pairs[m]) for m in batches]
+        grad_source = jnp.stack([finish_of(m, dmids[m], grad_query[m], grad_pairs[m]) for m in batches])
 
     def gain_grad(gain, *both):
         terms = sum(jnp.sum(weight.astype(F32) * grad, axis=1) for weight, grad in both)
@@ -1145,7 +1139,7 @@
         feed_gain_grad = gain_grad(feed_gain, (gate_weight, gate_grad), (up_weight, up_grad))
     return (
         layer_out.reshape(tokens.shape),
-        jnp.stack(grad_source),
+        grad_source,
         query_grad,
         key_grad,
         value_grad,

time: 670 us -> 676 us (level)
    psum x4, waiting for transfers between devices: 24 us -> 35.1 us  [z_sum(): return lax.psum(value, 'rep', axis_index_groups=lines)]
    pallas_call x3, Pallas kernels: 117 us -> 126 us  [feed(): pl.pallas_call(lambda *refs: feed_kernel(*refs, sets=sets, pieces=len(par...]
    ppermute x64, waiting for transfers between devices: 34.9 us -> 27.8 us  [partner(): return lax.ppermute(value, axis, [(i, i ^ bit) for i in range(size)])]
    pallas_call x3 -> x2, Pallas kernels: 72.2 us -> 69.7 us  [attend_back(): pl.pallas_call(lambda *refs: back_kernel(*refs, m=m, blocks=blocks), grid...]
  transfers between devices with their start and end apart: 81 -> 81, of which waited for: 19 -> 17; matrix products, arithmetic and copies ran while one was open for 14% -> 13% of each run, Pallas kernels for 57% -> 58%
where the time goes in v1:
time: 676 us; the launch traced here: 665 us
  Pallas kernels  384 us (57%)
  waiting for transfers between devices  88.4 us (13%)
  other arithmetic  67.2 us (10%)
  starting transfers between devices  62.6 us (9%)
  local copies, waits for them, and re-layouts  47.1 us (7%)
  between operations  15.7 us (2%)
    pallas_call x3, Pallas kernels, feed(): pl.pallas_call(lambda *refs: feed_kernel(*refs, sets=sets, pieces=len(par...  126 us
    pallas_call x2, Pallas kernels, attend_back(): pl.pallas_call(lambda *refs: back_kernel(*refs, m=m, blocks=blocks), grid...  69.7 us
    pallas_call x2, Pallas kernels, attend(): pl.pallas_call(lambda *refs: attend_kernel(*refs, m=m, blocks=blocks), gr...  61.5 us
    ppermute x64, starting transfers between devices, partner(): return lax.ppermute(value, axis, [(i, i ^ bit) for i in range(size)])  42.3 us
    psum x4, waiting for transfers between devices, z_sum(): return lax.psum(value, 'rep', axis_index_groups=lines)  35.1 us
    ppermute x64, waiting for transfers between devices, partner(): return lax.ppermute(value, axis, [(i, i ^ bit) for i in range(size)])  27.8 us
    ppermute x10, waiting for transfers between devices, deal(): lax.ppermute(held, ('rep', 'shard'), pairs)  23.2 us
    pallas_call x2, Pallas kernels, output(): pl.pallas_call(lambda *refs: output_kernel(*refs, parts=len(hids), adds=l...  21.1 us
  transfers between devices with their start and end apart: 81, of which 17 were waited for; matrix products, arithmetic and copies ran while one was open for 13% of the time, Pallas kernels for 58%

profile of v1, /device:TPU:1, one launch (start us, length us, event | category | flops | bytes accessed | tf_op | source)
XLA Modules:
  0.0 665.4 jit_solution(5324196658413885763)
XLA Ops:
  20.4 4.6 prepare.1.refs_1_
  29.2 5.4 project.2
  36.5 9.6 %collective-permute-done.7.refs_5_ = bf16[320,1280]{1,0:T(8,128)(2,1)} collective-permute-done((bf16[320,1280]{1,0:T(8,128)(2,1)}, bf16[320,1280]{1,0:T(8,128)(2,1)}, u32[]{:S(2)}, u32[]{:S(2)}) %collective-permute-start.7) | collective-permute-done | bytes 819232 | tf_op jit(solution)/shard_map/ppermute | solution.py:630
  51.7 6.1 collective-permute-done.6.refs_3_.refs_7_.refs_10_.refs_14_
  61.2 7.8 %project.3 = (bf16[1280,1024]{1,0:T(8,128)(2,1)}, bf16[1280,1280]{1,0:T(8,128)(2,1)}) custom-call(s32[4]{0:T(128)} %pad_add_fusion.2.refs_0_, bf16[1280,1024]{1,0:T(8,128)(2,1)} %prepare.1.refs_1_, f32[32,1024]{1,0:T(8,128)} %get-tuple-element.458.refs_2_.refs_1_, f32[32,1024]{1,0:T(8,128)} %get-tuple-element.457.refs_3_.refs_2_, bf16[320,1280]{1,0:T(8,128)(2,1)} %refs_4_.2, ...), custom_call_target="tpu_custom_call" | custom-call | flops 3355443200 | bytes 9830400 | tf_op jit(solution)/shard_map/project/pallas_call | solution.py:212
  69.1 30.9 %attend.2 = (bf16[1280,512]{1,0:T(8,128)(2,1)}, f32[5,4,512]{2,1,0:T(4,128)}) custom-call(s32[2,4]{1,0:T(2,128)} %subtract_multiply_fusion.refs_0_, bf16[1280,1024]{1,0:T(8,128)(2,1)} %get-tuple-element.203.refs_1_.refs_5_, bf16[640,256]{1,0:T(8,128)(2,1)} %get-tuple-element.440.refs_2_.refs_6_.refs_9_.refs_13_, ...), custom_call_target="tpu_custom_call" | custom-call | flops 30000001024 | bytes 5000000 | tf_op jit(solution)/shard_map/attend/pallas_call | solution.py:56
  118.6 30.6 %attend.3 = (bf16[1280,512]{1,0:T(8,128)(2,1)}, f32[5,4,512]{2,1,0:T(4,128)}) custom-call(s32[2,4]{1,0:T(2,128)} %subtract_multiply_fusion.refs_0_, bf16[1280,1024]{1,0:T(8,128)(2,1)} %get-tuple-element.203.refs_1_.refs_5_, bf16[640,256]{1,0:T(8,128)(2,1)} %get-tuple-element.439.refs_2_.refs_6_.refs_9_.refs_13_, ...), custom_call_target="tpu_custom_call" | custom-call | flops 30000001024 | bytes 5000000 | tf_op jit(solution)/shard_map/attend/pallas_call | solution.py:56
  150.8 8.0 %merge.2 = (f32[512,1280]{1,0:T(8,128)}, bf16[512,1280]{1,0:T(8,128)(2,1)}, bf16[1280,1280]{1,0:T(8,128)(2,1)}) custom-call(s32[4]{0:T(128)} %pad_add_fusion.2.refs_0_, bf16[1280,512]{1,0:T(8,128)(2,1)} %get-tuple-element.217.refs_1_.refs_6_, bf16[1024,1280]{1,0:T(8,128)(2,1)} %bitcast.221, f32[1,1280]{1,0:T(1,128)} %get-tuple-element.455.refs_3_.gain_ref, ...), custom_call_target="tpu_custom_call" | custom-call | flops 1677721600 | bytes 16000000 | tf_op jit(solution)/shard_map/merge/pallas_call | solution.py:368
  158.8 6.7 %merge.3 = (f32[512,1280]{1,0:T(8,128)}, bf16[512,1280]{1,0:T(8,128)(2,1)}) custom-call(s32[4]{0:T(128)} %pad_add_fusion.2.refs_0_, bf16[1280,512]{1,0:T(8,128)(2,1)} %get-tuple-element.216.refs_1_.refs_2_.refs_6_, bf16[1024,1280]{1,0:T(8,128)(2,1)} %bitcast.222, f32[1,1280]{1,0:T(1,128)} %get-tuple-element.455.refs_3_.gain_ref, ...), custom_call_target="tpu_custom_call" | custom-call | flops 1677721600 | bytes 16000000 | tf_op jit(solution)/shard_map/merge/pallas_call | solution.py:368
  171.8 44.2 %feed.3 = (bf16[3,640,512]{2,1,0:T(8,128)(2,1)}, bf16[3,640,512]{2,1,0:T(8,128)(2,1)}, bf16[512,1280]{1,0:T(8,128)(2,1)}, bf16[512,1280]{1,0:T(8,128)(2,1)}, bf1...) custom-call(s32[2]{0:T(128)} %pad_add_fusion.1.refs_0_.refs_1_, ...), custom_call_target="tpu_custom_call" | custom-call | flops 21474836480 | bytes 40632320 | tf_op jit(solution)/shard_map/feed/pallas_call | solution.py:298
  218.2 46.8 %feed.4 = (bf16[2,640,768]{2,1,0:T(8,128)(2,1)}, bf16[1,640,768]{2,1,0:T(8,128)(2,1)}, bf16[2,640,768]{2,1,0:T(8,128)(2,1)}, bf16[1,640,768]{2,1,0:T(8,128)(2,1)...) custom-call(s32[2]{0:T(128)} %pad_add_fusion.1.refs_0_.refs_1_, ...), custom_call_target="tpu_custom_call" | custom-call | flops 32212254720 | bytes 45219840 | tf_op jit(solution)/shard_map/feed/pallas_call | solution.py:298
  269.0 35.2 %feed.5 = (bf16[3,640,512]{2,1,0:T(8,128)(2,1)}, bf16[3,640,512]{2,1,0:T(8,128)(2,1)}, bf16[512,1280]{1,0:T(8,128)(2,1)}, bf16[512,1280]{1,0:T(8,128)(2,1)}, bf1...) custom-call(s32[2]{0:T(128)} %pad_add_fusion.1.refs_0_.refs_1_, ...), custom_call_target="tpu_custom_call" | custom-call | flops 21474836480 | bytes 40632320 | tf_op jit(solution)/shard_map/feed/pallas_call | solution.py:298
  304.2 6.2 collective-permute-done.30
  321.8 9.0 %unmerge.2 = (bf16[512,1280]{1,0:T(8,128)(2,1)}, bf16[1280,512]{1,0:T(8,128)(2,1)}) custom-call(f32[512,1280]{1,0:T(8,128)} %get-tuple-element.255.mid_ref.refs_7_, bf16[1024,1280]{1,0:T(8,128)(2,1)} %bitcast.232, f32[1,1280]{1,0:T(1,128)} %get-tuple-element.455.refs_3_.gain_ref, bf16[1280,1280]{1,0:T(8,128)(2,1)} %get-tuple-element.221.refs_4_.whole_ref, ...), custom_call_target="tpu_custom_call" | custom-call | flops 1677721600 | bytes 16000000 | tf_op jit(solution)/shard_map/unmerge/pallas_call | solution.py:407
  330.8 9.4 %output.2 = bf16[1024,1280]{1,0:T(8,128)(2,1)} custom-call(bf16[2048,512]{1,0:T(8,128)(2,1)} %get-tuple-element.225.refs_0_, bf16[2048,768]{1,0:T(8,128)(2,1)} %get-tuple-element.234.refs_1_, bf16[2048,512]{1,0:T(8,128)(2,1)} %get-tuple-element.262.refs_2_, bf16[1280,512]{1,0:T(8,128)(2,1)} %get-tuple-element.263.refs_3_, ...), custom_call_target="tpu_custom_call" | custom-call | flops 5000000000 | bytes 16000000 | tf_op jit(solution)/shard_map/output/pallas_call | solution.py:513
  350.0 34.8 %attend_back.2 = (bf16[1280,512]{1,0:T(8,128)(2,1)}, bf16[4,2,5,64,256]{4,3,2,1,0:T(8,128)(2,1)}, bf16[2,5,64,256]{3,2,1,0:T(8,128)(2,1)}) custom-call(s32[2,4]{1,0:T(2,128)} %subtract_multiply_fusion.refs_0_, f32[32,1024]{1,0:T(8,128)} %get-tuple-element.458.refs_2_.refs_1_, f32[32,1024]{1,0:T(8,128)} %get-tuple-element.457.refs_3_.refs_2_, ...), custom_call_target="tpu_custom_call" | custom-call | flops 10000000000 | bytes 5000000 | tf_op jit(solution)/shard_map/attend_back/pallas_call | solution.py:146
  390.3 6.7 %all-reduce.5.cloned.1.call-done = bf16[3,320,512]{2,1,0:T(8,128)(2,1)} async-done(((bf16[3,320,512]{2,1,0:T(8,128)(2,1)}), bf16[3,320,512]{2,1,0:T(8,128)(2,1)}) %all-reduce.5.cloned.1.call-update) | async-done | bytes 983056 | tf_op jit(solution)/shard_map/psum | solution.py:706
  404.4 9.0 %unmerge.3 = (bf16[512,1280]{1,0:T(8,128)(2,1)}, bf16[1280,512]{1,0:T(8,128)(2,1)}) custom-call(f32[512,1280]{1,0:T(8,128)} %get-tuple-element.284.mid_ref.refs_8_, bf16[1024,1280]{1,0:T(8,128)(2,1)} %bitcast.233, f32[1,1280]{1,0:T(1,128)} %get-tuple-element.455.refs_3_.gain_ref, bf16[1280,1280]{1,0:T(8,128)(2,1)} %get-tuple-element.221.refs_4_.whole_ref, ...), custom_call_target="tpu_custom_call" | custom-call | flops 1677721600 | bytes 16000000 | tf_op jit(solution)/shard_map/unmerge/pallas_call | solution.py:407
  425.1 9.0 %grad_terms.1 = (bf16[640,640]{1,0:T(8,128)(2,1)}, bf16[640,640]{1,0:T(8,128)(2,1)}) custom-call(s32[2]{0:T(128)} %pad_add_fusion.1.refs_0_.refs_1_, bf16[1280,512]{1,0:T(8,128)(2,1)} %get-tuple-element.217.refs_1_.refs_6_, bf16[1280,512]{1,0:T(8,128)(2,1)} %get-tuple-element.216.refs_1_.refs_2_.refs_6_, bf16[1280,512]{1,0:T(8,128)(2,1)} %collective-permute-done.45.refs_3_, ...), custom_call_target="tpu_custom_call" | custom-call | flops 3355443200 | bytes 8000000 | tf_op jit(solution)/shard_map/grad_terms/pallas_call | solution.py:450
  435.6 34.8 %attend_back.3 = (bf16[1280,512]{1,0:T(8,128)(2,1)}, bf16[4,2,5,64,256]{4,3,2,1,0:T(8,128)(2,1)}, bf16[2,5,64,256]{3,2,1,0:T(8,128)(2,1)}) custom-call(s32[2,4]{1,0:T(2,128)} %subtract_multiply_fusion.refs_0_, f32[32,1024]{1,0:T(8,128)} %get-tuple-element.458.refs_2_.refs_1_, f32[32,1024]{1,0:T(8,128)} %get-tuple-element.457.refs_3_.refs_2_, ...), custom_call_target="tpu_custom_call" | custom-call | flops 10000000000 | bytes 5000000 | tf_op jit(solution)/shard_map/attend_back/pallas_call | solution.py:146
  474.2 11.0 %all-reduce.7.cloned.1.call-done = bf16[3,320,768]{2,1,0:T(8,128)(2,1)} async-done(((bf16[3,320,768]{2,1,0:T(8,128)(2,1)}), bf16[3,320,768]{2,1,0:T(8,128)(2,1)}) %all-reduce.7.cloned.1.call-update) | async-done | bytes 1474576 | tf_op jit(solution)/shard_map/psum | solution.py:706
  510.0 14.8 %joint_terms.1 = (bf16[640,960]{1,0:T(8,128)(2,1)}, bf16[640,960]{1,0:T(8,128)(2,1)}) custom-call(s32[2]{0:T(128)} %pad_add_fusion.1.refs_0_.refs_1_, bf16[1280,1024]{1,0:T(8,128)(2,1)} %prepare.1.refs_1_, bf16[1280,1024]{1,0:T(8,128)(2,1)} %collective-permute-done.58.refs_2_, bf16[1280,512]{1,0:T(8,128)(2,1)} %pad_maximum_fusion.9.refs_3_, ...), custom_call_target="tpu_custom_call" | custom-call | flops 6000000000 | bytes 14000000 | tf_op jit(solution)/shard_map/joint_terms/pallas_call | solution.py:481
  530.5 8.7 %finish.2 = bf16[512,1280]{1,0:T(8,128)(2,1)} custom-call(bf16[1024,1280]{1,0:T(8,128)(2,1)} %bitcast.223, f32[1,1280]{1,0:T(1,128)} %get-tuple-element.456.gain_ref, bf16[512,1280]{1,0:T(8,128)(2,1)} %get-tuple-element.293.dmid_ref, bf16[1280,512]{1,0:T(8,128)(2,1)} %get-tuple-element.341.dq_ref, bf16[640,512]{1,0:T(8,128)(2,1)} %bitcast.240, ...), custom_call_target="tpu_custom_call" | custom-call | flops 2516582400 | bytes 12000000 | tf_op jit(solution)/shard_map/finish/pallas_call | solution.py:541
  539.2 11.0 %all-reduce.9.cloned.1.call-done = bf16[3,320,512]{2,1,0:T(8,128)(2,1)} async-done(((bf16[3,320,512]{2,1,0:T(8,128)(2,1)}), bf16[3,320,512]{2,1,0:T(8,128)(2,1)}) %all-reduce.9.cloned.1.call-update) | async-done | bytes 983056 | tf_op jit(solution)/shard_map/psum | solution.py:706
  551.1 8.4 %finish.3 = bf16[512,1280]{1,0:T(8,128)(2,1)} custom-call(bf16[1024,1280]{1,0:T(8,128)(2,1)} %bitcast.224, f32[1,1280]{1,0:T(1,128)} %get-tuple-element.456.gain_ref, bf16[512,1280]{1,0:T(8,128)(2,1)} %get-tuple-element.294.dmid_ref, bf16[1280,512]{1,0:T(8,128)(2,1)} %get-tuple-element.347.dq_ref, bf16[640,512]{1,0:T(8,128)(2,1)} %bitcast.241, ...), custom_call_target="tpu_custom_call" | custom-call | flops 2516582400 | bytes 12000000 | tf_op jit(solution)/shard_map/finish/pallas_call | solution.py:541
  567.2 11.7 %output.3 = bf16[1024,1280]{1,0:T(8,128)(2,1)} custom-call(bf16[2048,512]{1,0:T(8,128)(2,1)} %get-tuple-element.225.refs_0_, bf16[2048,768]{1,0:T(8,128)(2,1)} %get-tuple-element.234.refs_1_, bf16[2048,512]{1,0:T(8,128)(2,1)} %get-tuple-element.262.refs_2_, bf16[1280,512]{1,0:T(8,128)(2,1)} %get-tuple-element.263.refs_3_, ...), custom_call_target="tpu_custom_call" | custom-call | flops 5000000000 | bytes 16000000 | tf_op jit(solution)/shard_map/output/pallas_call | solution.py:513
  594.3 7.0 %collective-permute-done.68 = bf16[3,320,512]{2,1,0:T(8,128)(2,1)} collective-permute-done((bf16[3,320,512]{2,1,0:T(8,128)(2,1)S(1)}, bf16[3,320,512]{2,1,0:T(8,128)(2,1)}, u32[]{:S(2)}, u32[]{:S(2)}) %collective-permute-start.68) | collective-permute-done | bytes 983072 | tf_op jit(solution)/shard_map/ppermute | solution.py:719
  608.5 14.6 %widen.1 = (f32[320,3584]{1,0:T(8,128)}, f32[320,3584]{1,0:T(8,128)}, f32[320,3584]{1,0:T(8,128)}, f32[320,1]{1,0:T(8,128)}) custom-call(s32[1]{0:T(128)} %bitcast.101.refs_0_, bf16[3,320,512]{2,1,0:T(8,128)(2,1)} %get-tuple-element.446.refs_1_, bf16[3,320,768]{2,1,0:T(8,128)(2,1)} %get-tuple-element.422.refs_2_, ...), custom_call_target="tpu_custom_call" | custom-call | bytes 26000000 | tf_op jit(solution)/shard_map/widen/pallas_call | solution.py:609
  623.3 4.6 collective-permute-start.71
  629.0 6.4 all-reduce.11.cloned.1.call-done
  642.3 6.9 %collective-permute-done.72 = bf16[1,320,960]{2,1,0:T(8,128)(2,1)S(1)} collective-permute-done((bf16[1,320,960]{2,1,0:T(8,128)(2,1)}, bf16[1,320,960]{2,1,0:T(8,128)(2,1)S(1)}, u32[]{:S(2)}, u32[]{:S(2)}) %collective-permute-start.72) | collective-permute-done | bytes 614432 | tf_op jit(solution)/shard_map/ppermute | solution.py:719
  649.3 4.5 collective-permute-done.73
  (376 shorter events, 185.3 us)
Async XLA Ops:
  7.2 163.6 %all-gather.4.cloned.1.call-start = ((), (), s32[]{:S(2)}) async-start(), calls=%async_computation | async-start | bytes 2211840 | tf_op jit(solution)/shard_map/all_gather | solution.py:702
  13.7 46.0 %collective-permute-start.8 = (bf16[320,1280]{1,0:T(8,128)(2,1)}, bf16[320,1280]{1,0:T(8,128)(2,1)}, u32[]{:S(2)}, u32[]{:S(2)}) collective-permute-start(bf16[320,1280]{1,0:T(8,128)(2,1)} %refs_4_.2), channel_id=1, source_target_pairs={{0,1},{1,0},{2,3},{3,2},{4,5},{5,4},{6,7},{7,6},{8,9},{9,8},{10,11... | collective-permute-start | bytes 2457608 | tf_op jit(solution)/shard_map/ppermute | solution.py:630
  49.9 50.1 %collective-permute-start.13 = (bf16[640,256]{1,0:T(8,128)(2,1)}, bf16[640,256]{1,0:T(8,128)(2,1)}, u32[]{:S(2)}, u32[]{:S(2)}) collective-permute-start(bf16[640,256]{1,0:T(8,128)(2,1)} %get-tuple-element.439.refs_2_.refs_6_.refs_9_.refs_13_), channel_id=1, source_target_pairs={{0,2},{1,3},{2,0},{3,1},{4,6},{5,7},{6,4},{7,5},{8,10},{9,11},{10,... | collective-permute-start | bytes 983048 | tf_op jit(solution)/shard_map/ppermute | solution.py:630
  59.7 40.3 %collective-permute-start.12 = (bf16[320,1280]{1,0:T(8,128)(2,1)}, bf16[320,1280]{1,0:T(8,128)(2,1)}, u32[]{:S(2)}, u32[]{:S(2)}) collective-permute-start(bf16[320,1280]{1,0:T(8,128)(2,1)} %refs_4_.3), channel_id=1, source_target_pairs={{0,2},{1,3},{2,0},{3,1},{4,6},{5,7},{6,4},{7,5},{8,10},{9,11},{10,... | collective-permute-start | bytes 2457608 | tf_op jit(solution)/shard_map/ppermute | solution.py:630
  61.1 38.8 %collective-permute-start.15 = (bf16[240,512]{1,0:T(8,128)(2,1)}, bf16[240,512]{1,0:T(8,128)(2,1)}, u32[]{:S(2)}, u32[]{:S(2)}) collective-permute-start(bf16[240,512]{1,0:T(8,128)(2,1)} %constant_dynamic-slice_fusion.18), channel_id=1, source_target_pairs={{0,2},{1,3},{2,0},{3,1},{4,6},{5,7},{6,4},{7,5},{8,10},{9,11},{10,... | collective-permute-start | bytes 737288 | tf_op jit(solution)/shard_map/ppermute | solution.py:630
  109.3 39.9 %collective-permute-start.22 = (bf16[320,1280]{1,0:T(8,128)(2,1)}, bf16[320,1280]{1,0:T(8,128)(2,1)}, u32[]{:S(2)}, u32[]{:S(2)}) collective-permute-start(bf16[320,1280]{1,0:T(8,128)(2,1)} %refs_4_.3), channel_id=1, source_target_pairs={{0,1},{1,0},{2,3},{3,2},{4,5},{5,4},{6,7},{7,6},{8,9},{9,8},{10,11... | collective-permute-start | bytes 2457608 | tf_op jit(solution)/shard_map/ppermute | solution.py:630
  110.3 107.9 %all-gather.6.cloned.1.call-start = ((), (), s32[]{:S(2)}) async-start(), calls=%async_computation.1 | async-start | bytes 3317760 | tf_op jit(solution)/shard_map/all_gather | solution.py:702
  110.6 38.7 %collective-permute-start.23 = (bf16[320,1280]{1,0:T(8,128)(2,1)}, bf16[320,1280]{1,0:T(8,128)(2,1)}, u32[]{:S(2)}, u32[]{:S(2)}) collective-permute-start(bf16[320,1280]{1,0:T(8,128)(2,1)} %collective-permute-done.12.refs_5_), channel_id=1, source_target_pairs={{0,1},{1,0},{2,3},{3,2},{4,5},{5,4},{6,7},{7,6},{8,9},{9,8},{10,11... | collective-permute-start | bytes 2457608 | tf_op jit(solution)/shard_map/ppermute | solution.py:630
  114.7 34.5 %collective-permute-start.21 = (bf16[240,512]{1,0:T(8,128)(2,1)S(1)}, bf16[240,512]{1,0:T(8,128)(2,1)S(1)}, u32[]{:S(2)}, u32[]{:S(2)}) collective-permute-start(bf16[240,512]{1,0:T(8,128)(2,1)S(1)} %constant_dynamic-slice_fusion.16), channel_id=1, source_target_pairs={{0,2},{1,3},{2,0},{3,1},{4,6},{5,7},{6,4},{7,5},{8,10},{9,11},{10,... | collective-permute-start | bytes 737288 | tf_op jit(solution)/shard_map/ppermute | solution.py:630
  150.1 118.9 %all-gather.8.cloned.1.call-start = ((), (), s32[]{:S(2)}) async-start(), calls=%async_computation.2 | async-start | bytes 2211840 | tf_op jit(solution)/shard_map/all_gather | solution.py:702
  169.1 47.0 %collective-permute-start.27 = (bf16[1280,512]{1,0:T(8,128)(2,1)}, bf16[1280,512]{1,0:T(8,128)(2,1)}, u32[]{:S(2)}, u32[]{:S(2)}) collective-permute-start(bf16[1280,512]{1,0:T(8,128)(2,1)} %pad_maximum_fusion.9.refs_3_), channel_id=1, source_target_pairs={{0,2},{1,3},{2,0},{3,1},{4,6},{5,7},{6,4},{7,5},{8,10},{9,11},{10,... | collective-permute-start | bytes 3932168 | tf_op jit(solution)/shard_map/ppermute | solution.py:630
  170.7 226.3 %all-reduce.5.cloned.1.call-start = ((), (), s32[]{:S(2)}) async-start(), calls=%async_computation.3 | async-start | bytes 1966080 | tf_op jit(solution)/shard_map/psum | solution.py:706
  216.0 49.1 %collective-permute-start.28 = (bf16[1920,512]{1,0:T(8,128)(2,1)}, bf16[1920,512]{1,0:T(8,128)(2,1)}, u32[]{:S(2)}, u32[]{:S(2)}) collective-permute-start(bf16[1920,512]{1,0:T(8,128)(2,1)} %bitcast.285), channel_id=1, source_target_pairs={{0,2},{1,3},{2,0},{3,1},{4,6},{5,7},{6,4},{7,5},{8,10},{9,11},{10,... | collective-permute-start | bytes 5898248 | tf_op jit(solution)/shard_map/ppermute | solution.py:630
  267.5 36.7 %collective-permute-start.29 = (bf16[3,320,512]{2,1,0:T(8,128)(2,1)}, bf16[3,320,512]{2,1,0:T(8,128)(2,1)}, u32[]{:S(2)}, u32[]{:S(2)}) collective-permute-start(bf16[3,320,512]{2,1,0:T(8,128)(2,1)} %fusion.6), channel_id=1, source_target_pairs={{0,4},{4,0},{8,12},{12,8},{16,20},{20,16},{24,28},{28,24},{1,5},{5... | collective-permute-start | bytes 2949128 | tf_op jit(solution)/shard_map/ppermute | solution.py:630
  267.8 42.6 %collective-permute-start.30 = (bf16[1280,768]{1,0:T(8,128)(2,1)}, bf16[1280,768]{1,0:T(8,128)(2,1)}, u32[]{:S(2)}, u32[]{:S(2)}) collective-permute-start(bf16[1280,768]{1,0:T(8,128)(2,1)} %bitcast.57), channel_id=1, source_target_pairs={{0,2},{1,3},{2,0},{3,1},{4,6},{5,7},{6,4},{7,5},{8,10},{9,11},{10,... | collective-permute-start | bytes 5898248 | tf_op jit(solution)/shard_map/ppermute | solution.py:630
  343.8 53.2 %collective-permute-start.37 = (bf16[1024,1280]{1,0:T(8,128)(2,1)}, bf16[1024,1280]{1,0:T(8,128)(2,1)}, u32[]{:S(2)}, u32[]{:S(2)}) collective-permute-start(bf16[1024,1280]{1,0:T(8,128)(2,1)} %output.2), channel_id=1, source_target_pairs={{0,1},{1,0},{2,3},{3,2},{4,5},{5,4},{6,7},{7,6},{8,9},{9,8},{10,11... | collective-permute-start | bytes 7864328 | tf_op jit(solution)/shard_map/ppermute | solution.py:630
  347.1 53.8 %collective-permute-start.39 = (bf16[512,1280]{1,0:T(8,128)(2,1)}, bf16[512,1280]{1,0:T(8,128)(2,1)}, u32[]{:S(2)}, u32[]{:S(2)}) collective-permute-start(bf16[512,1280]{1,0:T(8,128)(2,1)} %get-tuple-element.286), channel_id=1, source_target_pairs={{0,1},{1,0},{2,3},{3,2},{4,5},{5,4},{6,7},{7,6},{8,9},{9,8},{10,11... | collective-permute-start | bytes 3932168 | tf_op jit(solution)/shard_map/ppermute | solution.py:630
  347.1 56.7 %collective-permute-start.40 = (bf16[512,1280]{1,0:T(8,128)(2,1)}, bf16[512,1280]{1,0:T(8,128)(2,1)}, u32[]{:S(2)}, u32[]{:S(2)}) collective-permute-start(bf16[512,1280]{1,0:T(8,128)(2,1)} %get-tuple-element.288), channel_id=1, source_target_pairs={{0,1},{1,0},{2,3},{3,2},{4,5},{5,4},{6,7},{7,6},{8,9},{9,8},{10,11... | collective-permute-start | bytes 3932168 | tf_op jit(solution)/shard_map/ppermute | solution.py:630
  347.6 137.6 %all-reduce.7.cloned.1.call-start = ((), (), s32[]{:S(2)}) async-start(), calls=%async_computation.4 | async-start | bytes 2949120 | tf_op jit(solution)/shard_map/psum | solution.py:706
  348.6 38.0 %collective-permute-start.36 = (bf16[1,320,768]{2,1,0:T(8,128)(2,1)}, bf16[1,320,768]{2,1,0:T(8,128)(2,1)}, u32[]{:S(2)}, u32[]{:S(2)}) collective-permute-start(bf16[1,320,768]{2,1,0:T(8,128)(2,1)} %fusion.16), channel_id=1, source_target_pairs={{0,4},{4,0},{8,12},{12,8},{16,20},{20,16},{24,28},{28,24},{1,5},{5... | collective-permute-start | bytes 1474568 | tf_op jit(solution)/shard_map/ppermute | solution.py:630
  348.8 67.2 %collective-permute-start.38 = (bf16[1920,512]{1,0:T(8,128)(2,1)}, bf16[1920,512]{1,0:T(8,128)(2,1)S(1)}, u32[]{:S(2)}, u32[]{:S(2)}) collective-permute-start(bf16[1920,512]{1,0:T(8,128)(2,1)} %bitcast.282), channel_id=1, source_target_pairs={{0,2},{1,3},{2,0},{3,1},{4,6},{5,7},{6,4},{7,5},{8,10},{9,11},{10,... | collective-permute-start | bytes 5898248 | tf_op jit(solution)/shard_map/ppermute | solution.py:630
  420.8 89.2 %collective-permute-start.58 = (bf16[1280,1024]{1,0:T(8,128)(2,1)}, bf16[1280,1024]{1,0:T(8,128)(2,1)}, u32[]{:S(2)}, u32[]{:S(2)}) collective-permute-start(bf16[1280,1024]{1,0:T(8,128)(2,1)} %prepare.1.refs_1_), channel_id=1, source_target_pairs={{0,1},{1,0},{2,3},{3,2},{4,5},{5,4},{6,7},{7,6},{8,9},{9,8},{10,11... | collective-permute-start | bytes 7864328 | tf_op jit(solution)/shard_map/ppermute | solution.py:630
  421.3 128.9 %all-reduce.9.cloned.1.call-start = ((), (), s32[]{:S(2)}) async-start(), calls=%async_computation.5 | async-start | bytes 1966080 | tf_op jit(solution)/shard_map/psum | solution.py:706
  422.7 62.5 %collective-permute-start.44 = (bf16[3,320,512]{2,1,0:T(8,128)(2,1)S(1)}, bf16[3,320,512]{2,1,0:T(8,128)(2,1)}, u32[]{:S(2)}, u32[]{:S(2)}) collective-permute-start(bf16[3,320,512]{2,1,0:T(8,128)(2,1)S(1)} %copy-done.26), channel_id=1, source_target_pairs={{0,4},{4,0},{8,12},{12,8},{16,20},{20,16},{24,28},{28,24},{1,5},{5... | collective-permute-start | bytes 2949128 | tf_op jit(solution)/shard_map/ppermute | solution.py:630
  423.9 46.6 %collective-permute-start.50 = (bf16[2,5,64,256]{3,2,1,0:T(8,128)(2,1)S(1)}, bf16[2,5,64,256]{3,2,1,0:T(8,128)(2,1)}, u32[]{:S(2)}, u32[]{:S(2)}) collective-permute-start(bf16[2,5,64,256]{3,2,1,0:T(8,128)(2,1)S(1)} %slice_bitcast_fusion.3), channel_id=1, source_target_pairs={{0,2},{1,3},{2,0},{3,1},{4,6},{5,7},{6,4},{7,5},{8,10},{9,11},{10,... | collective-permute-start | bytes 983048 | tf_op jit(solution)/shard_map/ppermute | solution.py:630
  434.0 51.2 %collective-permute-start.49 = (bf16[640,640]{1,0:T(8,128)(2,1)}, bf16[640,640]{1,0:T(8,128)(2,1)}, u32[]{:S(2)}, u32[]{:S(2)}) collective-permute-start(bf16[640,640]{1,0:T(8,128)(2,1)} %get-tuple-element.307), channel_id=1, source_target_pairs={{0,2},{1,3},{2,0},{3,1},{4,6},{5,7},{6,4},{7,5},{8,10},{9,11},{10,... | collective-permute-start | bytes 2457608 | tf_op jit(solution)/shard_map/ppermute | solution.py:630
  434.3 59.1 %collective-permute-start.55 = (bf16[3,320,512]{2,1,0:T(8,128)(2,1)}, bf16[3,320,512]{2,1,0:T(8,128)(2,1)}, u32[]{:S(2)}, u32[]{:S(2)}) collective-permute-start(bf16[3,320,512]{2,1,0:T(8,128)(2,1)} %all-reduce.5.cloned.1.call-done), channel_id=1, source_target_pairs={{0,4},{1,0},{2,6},{3,2},{4,5},{5,1},{6,7},{7,3},{8,12},{9,8},{10,1... | collective-permute-start | bytes 2949128 | tf_op jit(solution)/shard_map/ppermute | solution.py:719
  501.4 134.0 %all-reduce.11.cloned.1.call-start = ((), (), s32[]{:S(2)}) async-start(), calls=%async_computation.6 | async-start | bytes 1310720 | tf_op jit(solution)/shard_map/psum | solution.py:706
  506.3 53.2 %collective-permute-start.63 = (bf16[3,320,768]{2,1,0:T(8,128)(2,1)}, bf16[3,320,768]{2,1,0:T(8,128)(2,1)}, u32[]{:S(2)}, u32[]{:S(2)}) collective-permute-start(bf16[3,320,768]{2,1,0:T(8,128)(2,1)} %all-reduce.7.cloned.1.call-done), channel_id=1, source_target_pairs={{0,4},{1,0},{2,6},{3,2},{4,5},{5,1},{6,7},{7,3},{8,12},{9,8},{10,1... | collective-permute-start | bytes 4423688 | tf_op jit(solution)/shard_map/ppermute | solution.py:719
  506.6 52.9 %collective-permute-start.64 = (bf16[3,320,768]{2,1,0:T(8,128)(2,1)}, bf16[3,320,768]{2,1,0:T(8,128)(2,1)}, u32[]{:S(2)}, u32[]{:S(2)}) collective-permute-start(bf16[3,320,768]{2,1,0:T(8,128)(2,1)} %all-reduce.7.cloned.1.call-done), channel_id=1, source_target_pairs={{1,4},{3,6},{4,1},{6,3},{9,12},{11,14},{12,9},{14,11},{17,20},{19,... | collective-permute-start | bytes 4423688 | tf_op jit(solution)/shard_map/ppermute | solution.py:719
  528.2 31.3 %collective-permute-start.61 = (bf16[640,960]{0,1:T(8,128)(2,1)}, bf16[640,960]{0,1:T(8,128)(2,1)}, u32[]{:S(2)}, u32[]{:S(2)}) collective-permute-start(bf16[640,960]{0,1:T(8,128)(2,1)} %copy.88), channel_id=1, source_target_pairs={{0,2},{1,3},{2,0},{3,1},{4,6},{5,7},{6,4},{7,5},{8,10},{9,11},{10,... | collective-permute-start | bytes 3686408 | tf_op jit(solution)/shard_map/ppermute | solution.py:630
  586.4 36.8 %collective-permute-start.67 = (bf16[1,320,640]{2,1,0:T(8,128)(2,1)S(1)}, bf16[1,320,640]{2,1,0:T(8,128)(2,1)S(1)}, u32[]{:S(2)}, u32[]{:S(2)}) collective-permute-start(bf16[1,320,640]{2,1,0:T(8,128)(2,1)S(1)} %add_convert_fusion.8), channel_id=1, source_target_pairs={{0,16},{4,20},{8,24},{12,28},{16,0},{20,4},{24,8},{28,12},{1,17},{... | collective-permute-start | bytes 1228808 | tf_op jit(solution)/shard_map/ppermute | solution.py:630
  (101 other events, 1028.9 us)
Sparse Core Ops, SparseCore 0:
  110.5 47.5 all-gather.3
  160.8 57.3 all-gather.5
  220.4 47.0 all-gather.7
  347.7 49.1 all-reduce.4
  421.4 63.7 all-reduce.6
  501.5 48.5 all-reduce.8
  585.4 49.8 all-reduce.10

commit v2 on v0

--- a/solution.py
+++ b/solution.py
@@ -900,7 +900,7 @@
         eighth_1, eighth_2 = [net.feed_eighth(part) for part in feed_cores[1:]]
         output_pieces = [output_weight, output_across, net.core(output_weight), net.core(output_across)]
         mixed_1, log_1 = attend(after(gap, mixed_0), query, pairs[1], own_pairs, micro, 1)
-        mixed_1, eighth_1, eighth_2 = bind((mixed_1, eighth_1, eighth_2))
+        mixed_1, eighth_1, eighth_2, *output_pieces[2:] = bind((mixed_1, eighth_1, eighth_2, *output_pieces[2:]))
         feed_parts += [net.feed_parts(feed_cores[1], eighth_1), net.feed_parts(feed_cores[2], eighth_2)]
         mixed, log_total = [mixed_0, mixed_1], [log_0, log_1]
         mixed_all = mixed + [net.core(value) for value in mixed]
@@ -1093,10 +1093,12 @@
             gate_weight,
             up_weight,
         )
-        held_q, sums = settle([chain_o], held_q, sums)
-        got_q = net.deal(held_q)
+        grad_source = jnp.stack([source_0, source_1])
+        sums, grad_source = settle([chain_o], sums, grad_source)
         held_o = chain_o.total()
         got_o = net.deal(held_o)
+        held_q, *got_o = bind((held_q, *got_o))
+        got_q = net.deal(held_q)
         output_rows = [value[0] for value in net.dealt(held_o, got_o)]
         query_rows = [value[0] for value in net.dealt(held_q, got_q)]
         pair_rows = [value[:, head_width // 2 :] for value in query_rows]
@@ -1111,7 +1113,6 @@
         key_grad, value_grad = columns_of(pair_rows)
         down_grad = down_grad.T
         feed_gain_grad = sums[:, 0] / feed_gain.astype(F32)
-        grad_source = [source_0, source_1]
     else:
         grad_query, grad_pairs, dmids = [], [], []
         for m in batches:
@@ -1132,7 +1133,7 @@
         feed_grads = net.whole_sum(feed_terms[0][0].reshape(3, width, hidden_width), 1)
         gate_grad, up_grad, down_grad = feed_grads[0], feed_grads[1], feed_grads[2].T
         layer_out = output(hids, downs, [], middle, 0, rows)
-        grad_source = [finish_of(m, dmids[m], grad_query[m], grad_pairs[m]) for m in batches]
+        grad_source = jnp.stack([finish_of(m, dmids[m], grad_query[m], grad_pairs[m]) for m in batches])
 
     def gain_grad(gain, *both):
         terms = sum(jnp.sum(weight.astype(F32) * grad, axis=1) for weight, grad in both)
@@ -1145,7 +1146,7 @@
         feed_gain_grad = gain_grad(feed_gain, (gate_weight, gate_grad), (up_weight, up_grad))
     return (
         layer_out.reshape(tokens.shape),
-        jnp.stack(grad_source),
+        grad_source,
         query_grad,
         key_grad,
         value_grad,

time: 670 us -> 661 us (0.987)
    all_gather x3, waiting for transfers between devices: 4.32 us -> 11.1 us  [spread(): return lax.all_gather(eighth, 'rep', axis=0, tiled=True)]
  transfers between devices with their start and end apart: 81 -> 81, of which waited for: 19 -> 17; matrix products, arithmetic and copies ran while one was open for 14% -> 14% of each run, Pallas kernels for 57% -> 58%
where the time goes in v2:
time: 661 us; the launch traced here: 650 us
  Pallas kernels  378 us (57%)
  waiting for transfers between devices  81.1 us (12%)
  other arithmetic  67.7 us (10%)
  starting transfers between devices  59.8 us (9%)
  local copies, waits for them, and re-layouts  48.7 us (7%)
  between operations  15.5 us (2%)
    pallas_call x3, Pallas kernels, feed(): pl.pallas_call(lambda *refs: feed_kernel(*refs, sets=sets, pieces=len(par...  117 us
    pallas_call x3, Pallas kernels, attend_back(): pl.pallas_call(lambda *refs: back_kernel(*refs, m=m, blocks=blocks), grid...  72.1 us
    pallas_call x2, Pallas kernels, attend(): pl.pallas_call(lambda *refs: attend_kernel(*refs, m=m, blocks=blocks), gr...  61.4 us
    ppermute x64, starting transfers between devices, partner(): return lax.ppermute(value, axis, [(i, i ^ bit) for i in range(size)])  41 us
    ppermute x64, waiting for transfers between devices, partner(): return lax.ppermute(value, axis, [(i, i ^ bit) for i in range(size)])  28.5 us
    ppermute x10, waiting for transfers between devices, deal(): lax.ppermute(held, ('rep', 'shard'), pairs)  23.1 us
    pallas_call x2, Pallas kernels, output(): pl.pallas_call(lambda *refs: output_kernel(*refs, parts=len(hids), adds=l...  21.1 us
    ppermute x10, starting transfers between devices, deal(): lax.ppermute(held, ('rep', 'shard'), pairs)  18.3 us
  transfers between devices with their start and end apart: 81, of which 17 were waited for; matrix products, arithmetic and copies ran while one was open for 14% of the time, Pallas kernels for 58%

profile of v2, /device:TPU:1, one launch (start us, length us, event | category | flops | bytes accessed | tf_op | source)
XLA Modules:
  0.0 650.5 jit_solution(7053145027305892574)
XLA Ops:
  20.4 4.6 prepare.1.refs_1_
  29.3 5.4 project.2
  36.7 9.5 %collective-permute-done.7.refs_5_ = bf16[320,1280]{1,0:T(8,128)(2,1)} collective-permute-done((bf16[320,1280]{1,0:T(8,128)(2,1)}, bf16[320,1280]{1,0:T(8,128)(2,1)}, u32[]{:S(2)}, u32[]{:S(2)}) %collective-permute-start.7) | collective-permute-done | bytes 819232 | tf_op jit(solution)/shard_map/ppermute | solution.py:630
  51.7 6.1 collective-permute-done.6.refs_3_.refs_7_.refs_10_.refs_14_
  61.2 7.8 %project.3 = (bf16[1280,1024]{1,0:T(8,128)(2,1)}, bf16[1280,1280]{1,0:T(8,128)(2,1)}) custom-call(s32[4]{0:T(128)} %pad_add_fusion.2.refs_0_, bf16[1280,1024]{1,0:T(8,128)(2,1)} %prepare.1.refs_1_, f32[32,1024]{1,0:T(8,128)} %get-tuple-element.484.refs_2_.refs_1_, f32[32,1024]{1,0:T(8,128)} %get-tuple-element.483.refs_3_.refs_2_, bf16[320,1280]{1,0:T(8,128)(2,1)} %refs_4_.2, ...), custom_call_target="tpu_custom_call" | custom-call | flops 3355443200 | bytes 9830400 | tf_op jit(solution)/shard_map/project/pallas_call | solution.py:212
  69.1 30.8 %attend.2 = (bf16[1280,512]{1,0:T(8,128)(2,1)}, f32[5,4,512]{2,1,0:T(4,128)}) custom-call(s32[2,4]{1,0:T(2,128)} %subtract_multiply_fusion.refs_0_, bf16[1280,1024]{1,0:T(8,128)(2,1)} %get-tuple-element.216.refs_1_.refs_5_, bf16[640,256]{1,0:T(8,128)(2,1)} %get-tuple-element.466.refs_2_.refs_6_.refs_9_.refs_13_, ...), custom_call_target="tpu_custom_call" | custom-call | flops 30000001024 | bytes 5000000 | tf_op jit(solution)/shard_map/attend/pallas_call | solution.py:56
  118.5 30.6 %attend.3 = (bf16[1280,512]{1,0:T(8,128)(2,1)}, f32[5,4,512]{2,1,0:T(4,128)}) custom-call(s32[2,4]{1,0:T(2,128)} %subtract_multiply_fusion.refs_0_, bf16[1280,1024]{1,0:T(8,128)(2,1)} %get-tuple-element.216.refs_1_.refs_5_, bf16[640,256]{1,0:T(8,128)(2,1)} %get-tuple-element.465.refs_2_.refs_6_.refs_9_.refs_13_, ...), custom_call_target="tpu_custom_call" | custom-call | flops 30000001024 | bytes 5000000 | tf_op jit(solution)/shard_map/attend/pallas_call | solution.py:56
  150.8 8.0 %merge.2 = (f32[512,1280]{1,0:T(8,128)}, bf16[512,1280]{1,0:T(8,128)(2,1)}, bf16[1280,1280]{1,0:T(8,128)(2,1)}) custom-call(s32[4]{0:T(128)} %pad_add_fusion.2.refs_0_, bf16[1280,512]{1,0:T(8,128)(2,1)} %get-tuple-element.230.refs_1_.refs_6_, bf16[1024,1280]{1,0:T(8,128)(2,1)} %bitcast.221, f32[1,1280]{1,0:T(1,128)} %get-tuple-element.481.refs_3_.gain_ref, ...), custom_call_target="tpu_custom_call" | custom-call | flops 1677721600 | bytes 16000000 | tf_op jit(solution)/shard_map/merge/pallas_call | solution.py:368
  158.7 6.7 %merge.3 = (f32[512,1280]{1,0:T(8,128)}, bf16[512,1280]{1,0:T(8,128)(2,1)}) custom-call(s32[4]{0:T(128)} %pad_add_fusion.2.refs_0_, bf16[1280,512]{1,0:T(8,128)(2,1)} %get-tuple-element.229.refs_1_.refs_6_.refs_2_, bf16[1024,1280]{1,0:T(8,128)(2,1)} %bitcast.222, f32[1,1280]{1,0:T(1,128)} %get-tuple-element.481.refs_3_.gain_ref, ...), custom_call_target="tpu_custom_call" | custom-call | flops 1677721600 | bytes 16000000 | tf_op jit(solution)/shard_map/merge/pallas_call | solution.py:368
  171.8 35.2 %feed.3 = (bf16[3,640,512]{2,1,0:T(8,128)(2,1)}, bf16[3,640,512]{2,1,0:T(8,128)(2,1)}, bf16[512,1280]{1,0:T(8,128)(2,1)}, bf16[512,1280]{1,0:T(8,128)(2,1)}, bf1...) custom-call(s32[2]{0:T(128)} %pad_add_fusion.1.refs_0_.refs_1_, ...), custom_call_target="tpu_custom_call" | custom-call | flops 21474836480 | bytes 40632320 | tf_op jit(solution)/shard_map/feed/pallas_call | solution.py:298
  207.1 11.1 %all-gather.6.cloned.1.call-done = bf16[1920,768]{1,0:T(8,128)(2,1)} async-done(((bf16[240,768]{1,0:T(8,128)(2,1)}), bf16[1920,768]{1,0:T(8,128)(2,1)}) %all-gather.6.cloned.1.call-update) | async-done | bytes 2949136 | tf_op jit(solution)/shard_map/all_gather | solution.py:702
  218.2 46.8 %feed.4 = (bf16[2,640,768]{2,1,0:T(8,128)(2,1)}, bf16[1,640,768]{2,1,0:T(8,128)(2,1)}, bf16[2,640,768]{2,1,0:T(8,128)(2,1)}, bf16[1,640,768]{2,1,0:T(8,128)(2,1)...) custom-call(s32[2]{0:T(128)} %pad_add_fusion.1.refs_0_.refs_1_, ...), custom_call_target="tpu_custom_call" | custom-call | flops 32212254720 | bytes 45219840 | tf_op jit(solution)/shard_map/feed/pallas_call | solution.py:298
  268.9 35.1 %feed.5 = (bf16[3,640,512]{2,1,0:T(8,128)(2,1)}, bf16[3,640,512]{2,1,0:T(8,128)(2,1)}, bf16[512,1280]{1,0:T(8,128)(2,1)}, bf16[512,1280]{1,0:T(8,128)(2,1)}, bf1...) custom-call(s32[2]{0:T(128)} %pad_add_fusion.1.refs_0_.refs_1_, ...), custom_call_target="tpu_custom_call" | custom-call | flops 21474836480 | bytes 40632320 | tf_op jit(solution)/shard_map/feed/pallas_call | solution.py:298
  304.0 6.3 collective-permute-done.30
  324.5 9.0 %unmerge.2 = (bf16[512,1280]{1,0:T(8,128)(2,1)}, bf16[1280,512]{1,0:T(8,128)(2,1)}) custom-call(f32[512,1280]{1,0:T(8,128)} %get-tuple-element.268.mid_ref.refs_7_, bf16[1024,1280]{1,0:T(8,128)(2,1)} %bitcast.232, f32[1,1280]{1,0:T(1,128)} %get-tuple-element.481.refs_3_.gain_ref, bf16[1280,1280]{1,0:T(8,128)(2,1)} %get-tuple-element.234.refs_4_.whole_ref, ...), custom_call_target="tpu_custom_call" | custom-call | flops 1677721600 | bytes 16000000 | tf_op jit(solution)/shard_map/unmerge/pallas_call | solution.py:407
  333.6 9.4 %output.2 = bf16[1024,1280]{1,0:T(8,128)(2,1)} custom-call(bf16[2048,512]{1,0:T(8,128)(2,1)} %get-tuple-element.238.refs_0_, bf16[2048,768]{1,0:T(8,128)(2,1)} %get-tuple-element.247.refs_1_, bf16[2048,512]{1,0:T(8,128)(2,1)} %get-tuple-element.275.refs_2_, bf16[1280,512]{1,0:T(8,128)(2,1)} %get-tuple-element.276.refs_3_, ...), custom_call_target="tpu_custom_call" | custom-call | flops 5000000000 | bytes 16000000 | tf_op jit(solution)/shard_map/output/pallas_call | solution.py:513
  348.9 34.8 %attend_back.3 = (bf16[1280,512]{1,0:T(8,128)(2,1)}, bf16[4,2,5,64,256]{4,3,2,1,0:T(8,128)(2,1)}, bf16[2,5,64,256]{3,2,1,0:T(8,128)(2,1)}) custom-call(s32[2,4]{1,0:T(2,128)} %subtract_multiply_fusion.refs_0_, f32[32,1024]{1,0:T(8,128)} %get-tuple-element.484.refs_2_.refs_1_, f32[32,1024]{1,0:T(8,128)} %get-tuple-element.483.refs_3_.refs_2_, ...), custom_call_target="tpu_custom_call" | custom-call | flops 40000000000 | bytes 5000000 | tf_op jit(solution)/shard_map/attend_back/pallas_call | solution.py:146
  397.9 9.3 %unmerge.3 = (bf16[512,1280]{1,0:T(8,128)(2,1)}, bf16[1280,512]{1,0:T(8,128)(2,1)}) custom-call(f32[512,1280]{1,0:T(8,128)} %get-tuple-element.297.mid_ref.refs_8_, bf16[1024,1280]{1,0:T(8,128)(2,1)} %bitcast.233, f32[1,1280]{1,0:T(1,128)} %get-tuple-element.481.refs_3_.gain_ref, bf16[1280,1280]{1,0:T(8,128)(2,1)} %get-tuple-element.234.refs_4_.whole_ref, ...), custom_call_target="tpu_custom_call" | custom-call | flops 1677721600 | bytes 16000000 | tf_op jit(solution)/shard_map/unmerge/pallas_call | solution.py:407
  415.9 22.1 %attend_back.4 = (bf16[768,512]{1,0:T(8,128)(2,1)}, bf16[4,2,3,64,256]{4,3,2,1,0:T(8,128)(2,1)}, bf16[2,3,64,256]{3,2,1,0:T(8,128)(2,1)}) custom-call(s32[2,4]{1,0:T(2,128)} %subtract_multiply_fusion.refs_0_, f32[32,1024]{1,0:T(8,128)} %get-tuple-element.484.refs_2_.refs_1_, f32[32,1024]{1,0:T(8,128)} %get-tuple-element.483.refs_3_.refs_2_, ...), custom_call_target="tpu_custom_call" | custom-call | flops 24000000000 | bytes 3000000 | tf_op jit(solution)/shard_map/attend_back/pallas_call | solution.py:146
  442.5 8.7 %grad_terms.1 = (bf16[640,640]{1,0:T(8,128)(2,1)}, bf16[640,640]{1,0:T(8,128)(2,1)}) custom-call(s32[2]{0:T(128)} %pad_add_fusion.1.refs_0_.refs_1_, bf16[1280,512]{1,0:T(8,128)(2,1)} %get-tuple-element.230.refs_1_.refs_6_, bf16[1280,512]{1,0:T(8,128)(2,1)} %get-tuple-element.229.refs_1_.refs_6_.refs_2_, bf16[1280,512]{1,0:T(8,128)(2,1)} %collective-permute-done.46.refs_3_, ...), custom_call_target="tpu_custom_call" | custom-call | flops 3355443200 | bytes 8000000 | tf_op jit(solution)/shard_map/grad_terms/pallas_call | solution.py:450
  458.0 15.2 %attend_back.5 = (bf16[512,512]{1,0:T(8,128)(2,1)}, bf16[4,2,2,64,256]{4,3,2,1,0:T(8,128)(2,1)}, bf16[2,2,64,256]{3,2,1,0:T(8,128)(2,1)}) custom-call(s32[2,4]{1,0:T(2,128)} %subtract_multiply_fusion.refs_0_, f32[32,1024]{1,0:T(8,128)} %get-tuple-element.484.refs_2_.refs_1_, f32[32,1024]{1,0:T(8,128)} %get-tuple-element.483.refs_3_.refs_2_, ...), custom_call_target="tpu_custom_call" | custom-call | flops 16000000000 | bytes 2000000 | tf_op jit(solution)/shard_map/attend_back/pallas_call | solution.py:146
  494.8 15.0 %joint_terms.1 = (bf16[640,960]{1,0:T(8,128)(2,1)}, bf16[640,960]{1,0:T(8,128)(2,1)}) custom-call(s32[2]{0:T(128)} %pad_add_fusion.1.refs_0_.refs_1_, bf16[1280,1024]{1,0:T(8,128)(2,1)} %prepare.1.refs_1_, bf16[1280,1024]{1,0:T(8,128)(2,1)} %collective-permute-done.58.refs_2_, bf16[1280,512]{1,0:T(8,128)(2,1)} %pad_maximum_fusion.9.refs_3_, ...), custom_call_target="tpu_custom_call" | custom-call | flops 6000000000 | bytes 14000000 | tf_op jit(solution)/shard_map/joint_terms/pallas_call | solution.py:481
  515.0 8.6 %finish.2 = bf16[512,1280]{1,0:T(8,128)(2,1)} custom-call(bf16[1024,1280]{1,0:T(8,128)(2,1)} %bitcast.223, f32[1,1280]{1,0:T(1,128)} %get-tuple-element.482.gain_ref, bf16[512,1280]{1,0:T(8,128)(2,1)} %get-tuple-element.306.dmid_ref, bf16[1280,512]{1,0:T(8,128)(2,1)} %get-tuple-element.367.dq_ref, bf16[640,512]{1,0:T(8,128)(2,1)} %bitcast.240, ...), custom_call_target="tpu_custom_call" | custom-call | flops 2516582400 | bytes 12000000 | tf_op jit(solution)/shard_map/finish/pallas_call | solution.py:541
  523.6 11.8 %all-reduce.9.cloned.1.call-done = bf16[3,320,512]{2,1,0:T(8,128)(2,1)} async-done(((bf16[3,320,512]{2,1,0:T(8,128)(2,1)}), bf16[3,320,512]{2,1,0:T(8,128)(2,1)}) %all-reduce.9.cloned.1.call-update) | async-done | bytes 983056 | tf_op jit(solution)/shard_map/psum | solution.py:706
  536.4 8.4 %finish.3 = bf16[512,1280]{1,0:T(8,128)(2,1)} custom-call(bf16[1024,1280]{1,0:T(8,128)(2,1)} %bitcast.224, f32[1,1280]{1,0:T(1,128)} %get-tuple-element.482.gain_ref, bf16[512,1280]{1,0:T(8,128)(2,1)} %get-tuple-element.307.dmid_ref, bf16[1280,512]{1,0:T(8,128)(2,1)} %copy-done.1, bf16[640,512]{1,0:T(8,128)(2,1)} %bitcast.241, ...), custom_call_target="tpu_custom_call" | custom-call | flops 2516582400 | bytes 12000000 | tf_op jit(solution)/shard_map/finish/pallas_call | solution.py:541
  552.5 11.7 %output.3 = bf16[1024,1280]{1,0:T(8,128)(2,1)} custom-call(bf16[2048,512]{1,0:T(8,128)(2,1)} %get-tuple-element.238.refs_0_, bf16[2048,768]{1,0:T(8,128)(2,1)} %get-tuple-element.247.refs_1_, bf16[2048,512]{1,0:T(8,128)(2,1)} %get-tuple-element.275.refs_2_, bf16[1280,512]{1,0:T(8,128)(2,1)} %get-tuple-element.276.refs_3_, ...), custom_call_target="tpu_custom_call" | custom-call | flops 5000000000 | bytes 16000000 | tf_op jit(solution)/shard_map/output/pallas_call | solution.py:513
  579.6 7.0 %collective-permute-done.68 = bf16[3,320,512]{2,1,0:T(8,128)(2,1)} collective-permute-done((bf16[3,320,512]{2,1,0:T(8,128)(2,1)S(1)}, bf16[3,320,512]{2,1,0:T(8,128)(2,1)}, u32[]{:S(2)}, u32[]{:S(2)}) %collective-permute-start.68) | collective-permute-done | bytes 983072 | tf_op jit(solution)/shard_map/ppermute | solution.py:719
  593.8 14.6 %widen.1 = (f32[320,3584]{1,0:T(8,128)}, f32[320,3584]{1,0:T(8,128)}, f32[320,3584]{1,0:T(8,128)}, f32[320,1]{1,0:T(8,128)}) custom-call(s32[1]{0:T(128)} %bitcast.101.refs_0_, bf16[3,320,512]{2,1,0:T(8,128)(2,1)} %get-tuple-element.472.refs_1_, bf16[3,320,768]{2,1,0:T(8,128)(2,1)} %get-tuple-element.448.refs_2_, ...), custom_call_target="tpu_custom_call" | custom-call | bytes 26000000 | tf_op jit(solution)/shard_map/widen/pallas_call | solution.py:609
  608.6 4.6 collective-permute-start.71
  614.3 6.4 all-reduce.11.cloned.1.call-done
  627.6 6.9 %collective-permute-done.72 = bf16[1,320,960]{2,1,0:T(8,128)(2,1)S(1)} collective-permute-done((bf16[1,320,960]{2,1,0:T(8,128)(2,1)}, bf16[1,320,960]{2,1,0:T(8,128)(2,1)S(1)}, u32[]{:S(2)}, u32[]{:S(2)}) %collective-permute-start.72) | collective-permute-done | bytes 614432 | tf_op jit(solution)/shard_map/ppermute | solution.py:719
  634.5 4.5 collective-permute-done.73
  (368 shorter events, 182.9 us)
Async XLA Ops:
  7.2 163.6 %all-gather.4.cloned.1.call-start = ((), (), s32[]{:S(2)}) async-start(), calls=%async_computation | async-start | bytes 2211840 | tf_op jit(solution)/shard_map/all_gather | solution.py:702
  13.7 46.0 %collective-permute-start.8 = (bf16[320,1280]{1,0:T(8,128)(2,1)}, bf16[320,1280]{1,0:T(8,128)(2,1)}, u32[]{:S(2)}, u32[]{:S(2)}) collective-permute-start(bf16[320,1280]{1,0:T(8,128)(2,1)} %refs_4_.2), channel_id=1, source_target_pairs={{0,1},{1,0},{2,3},{3,2},{4,5},{5,4},{6,7},{7,6},{8,9},{9,8},{10,11... | collective-permute-start | bytes 2457608 | tf_op jit(solution)/shard_map/ppermute | solution.py:630
  49.9 50.0 %collective-permute-start.13 = (bf16[640,256]{1,0:T(8,128)(2,1)}, bf16[640,256]{1,0:T(8,128)(2,1)}, u32[]{:S(2)}, u32[]{:S(2)}) collective-permute-start(bf16[640,256]{1,0:T(8,128)(2,1)} %get-tuple-element.465.refs_2_.refs_6_.refs_9_.refs_13_), channel_id=1, source_target_pairs={{0,2},{1,3},{2,0},{3,1},{4,6},{5,7},{6,4},{7,5},{8,10},{9,11},{10,... | collective-permute-start | bytes 983048 | tf_op jit(solution)/shard_map/ppermute | solution.py:630
  59.7 40.2 %collective-permute-start.12 = (bf16[320,1280]{1,0:T(8,128)(2,1)}, bf16[320,1280]{1,0:T(8,128)(2,1)}, u32[]{:S(2)}, u32[]{:S(2)}) collective-permute-start(bf16[320,1280]{1,0:T(8,128)(2,1)} %refs_4_.3), channel_id=1, source_target_pairs={{0,2},{1,3},{2,0},{3,1},{4,6},{5,7},{6,4},{7,5},{8,10},{9,11},{10,... | collective-permute-start | bytes 2457608 | tf_op jit(solution)/shard_map/ppermute | solution.py:630
  61.2 38.7 %collective-permute-start.15 = (bf16[240,512]{1,0:T(8,128)(2,1)}, bf16[240,512]{1,0:T(8,128)(2,1)}, u32[]{:S(2)}, u32[]{:S(2)}) collective-permute-start(bf16[240,512]{1,0:T(8,128)(2,1)} %constant_dynamic-slice_fusion.18), channel_id=1, source_target_pairs={{0,2},{1,3},{2,0},{3,1},{4,6},{5,7},{6,4},{7,5},{8,10},{9,11},{10,... | collective-permute-start | bytes 737288 | tf_op jit(solution)/shard_map/ppermute | solution.py:630
  109.2 40.0 %collective-permute-start.22 = (bf16[320,1280]{1,0:T(8,128)(2,1)}, bf16[320,1280]{1,0:T(8,128)(2,1)}, u32[]{:S(2)}, u32[]{:S(2)}) collective-permute-start(bf16[320,1280]{1,0:T(8,128)(2,1)} %refs_4_.3), channel_id=1, source_target_pairs={{0,1},{1,0},{2,3},{3,2},{4,5},{5,4},{6,7},{7,6},{8,9},{9,8},{10,11... | collective-permute-start | bytes 2457608 | tf_op jit(solution)/shard_map/ppermute | solution.py:630
  110.3 107.9 %all-gather.6.cloned.1.call-start = ((), (), s32[]{:S(2)}) async-start(), calls=%async_computation.1 | async-start | bytes 3317760 | tf_op jit(solution)/shard_map/all_gather | solution.py:702
  110.5 38.7 %collective-permute-start.23 = (bf16[320,1280]{1,0:T(8,128)(2,1)}, bf16[320,1280]{1,0:T(8,128)(2,1)}, u32[]{:S(2)}, u32[]{:S(2)}) collective-permute-start(bf16[320,1280]{1,0:T(8,128)(2,1)} %collective-permute-done.12.refs_5_), channel_id=1, source_target_pairs={{0,1},{1,0},{2,3},{3,2},{4,5},{5,4},{6,7},{7,6},{8,9},{9,8},{10,11... | collective-permute-start | bytes 2457608 | tf_op jit(solution)/shard_map/ppermute | solution.py:630
  114.7 34.6 %collective-permute-start.21 = (bf16[240,512]{1,0:T(8,128)(2,1)S(1)}, bf16[240,512]{1,0:T(8,128)(2,1)S(1)}, u32[]{:S(2)}, u32[]{:S(2)}) collective-permute-start(bf16[240,512]{1,0:T(8,128)(2,1)S(1)} %constant_dynamic-slice_fusion.16), channel_id=1, source_target_pairs={{0,2},{1,3},{2,0},{3,1},{4,6},{5,7},{6,4},{7,5},{8,10},{9,11},{10,... | collective-permute-start | bytes 737288 | tf_op jit(solution)/shard_map/ppermute | solution.py:630
  118.5 30.8 %collective-permute-start.19 = (bf16[240,768]{1,0:T(8,128)(2,1)S(1)}, bf16[240,768]{1,0:T(8,128)(2,1)S(1)}, u32[]{:S(2)}, u32[]{:S(2)}) collective-permute-start(bf16[240,768]{1,0:T(8,128)(2,1)S(1)} %constant_dynamic-slice_fusion.17), channel_id=1, source_target_pairs={{0,2},{1,3},{2,0},{3,1},{4,6},{5,7},{6,4},{7,5},{8,10},{9,11},{10,... | collective-permute-start | bytes 1105928 | tf_op jit(solution)/shard_map/ppermute | solution.py:630
  150.1 118.8 %all-gather.8.cloned.1.call-start = ((), (), s32[]{:S(2)}) async-start(), calls=%async_computation.2 | async-start | bytes 2211840 | tf_op jit(solution)/shard_map/all_gather | solution.py:702
  169.1 38.0 %collective-permute-start.27 = (bf16[1280,512]{1,0:T(8,128)(2,1)}, bf16[1280,512]{1,0:T(8,128)(2,1)}, u32[]{:S(2)}, u32[]{:S(2)}) collective-permute-start(bf16[1280,512]{1,0:T(8,128)(2,1)} %pad_maximum_fusion.9.refs_3_), channel_id=1, source_target_pairs={{0,2},{1,3},{2,0},{3,1},{4,6},{5,7},{6,4},{7,5},{8,10},{9,11},{10,... | collective-permute-start | bytes 3932168 | tf_op jit(solution)/shard_map/ppermute | solution.py:630
  170.7 217.1 %all-reduce.5.cloned.1.call-start = ((), (), s32[]{:S(2)}) async-start(), calls=%async_computation.3 | async-start | bytes 1966080 | tf_op jit(solution)/shard_map/psum | solution.py:706
  207.0 57.9 %collective-permute-start.28 = (bf16[1920,512]{1,0:T(8,128)(2,1)}, bf16[1920,512]{1,0:T(8,128)(2,1)}, u32[]{:S(2)}, u32[]{:S(2)}) collective-permute-start(bf16[1920,512]{1,0:T(8,128)(2,1)} %bitcast.281), channel_id=1, source_target_pairs={{0,2},{1,3},{2,0},{3,1},{4,6},{5,7},{6,4},{7,5},{8,10},{9,11},{10,... | collective-permute-start | bytes 5898248 | tf_op jit(solution)/shard_map/ppermute | solution.py:630
  267.4 36.5 %collective-permute-start.29 = (bf16[3,320,512]{2,1,0:T(8,128)(2,1)}, bf16[3,320,512]{2,1,0:T(8,128)(2,1)}, u32[]{:S(2)}, u32[]{:S(2)}) collective-permute-start(bf16[3,320,512]{2,1,0:T(8,128)(2,1)} %fusion.6), channel_id=1, source_target_pairs={{0,4},{4,0},{8,12},{12,8},{16,20},{20,16},{24,28},{28,24},{1,5},{5... | collective-permute-start | bytes 2949128 | tf_op jit(solution)/shard_map/ppermute | solution.py:630
  267.7 42.6 %collective-permute-start.30 = (bf16[1280,768]{1,0:T(8,128)(2,1)}, bf16[1280,768]{1,0:T(8,128)(2,1)}, u32[]{:S(2)}, u32[]{:S(2)}) collective-permute-start(bf16[1280,768]{1,0:T(8,128)(2,1)} %bitcast.57), channel_id=1, source_target_pairs={{0,2},{1,3},{2,0},{3,1},{4,6},{5,7},{6,4},{7,5},{8,10},{9,11},{10,... | collective-permute-start | bytes 5898248 | tf_op jit(solution)/shard_map/ppermute | solution.py:630
  323.8 71.6 %collective-permute-start.39 = (bf16[512,1280]{1,0:T(8,128)(2,1)}, bf16[512,1280]{1,0:T(8,128)(2,1)}, u32[]{:S(2)}, u32[]{:S(2)}) collective-permute-start(bf16[512,1280]{1,0:T(8,128)(2,1)} %get-tuple-element.299), channel_id=1, source_target_pairs={{0,1},{1,0},{2,3},{3,2},{4,5},{5,4},{6,7},{7,6},{8,9},{9,8},{10,11... | collective-permute-start | bytes 3932168 | tf_op jit(solution)/shard_map/ppermute | solution.py:630
  324.5 72.9 %collective-permute-start.40 = (bf16[512,1280]{1,0:T(8,128)(2,1)}, bf16[512,1280]{1,0:T(8,128)(2,1)}, u32[]{:S(2)}, u32[]{:S(2)}) collective-permute-start(bf16[512,1280]{1,0:T(8,128)(2,1)} %get-tuple-element.301), channel_id=1, source_target_pairs={{0,1},{1,0},{2,3},{3,2},{4,5},{5,4},{6,7},{7,6},{8,9},{9,8},{10,11... | collective-permute-start | bytes 3932168 | tf_op jit(solution)/shard_map/ppermute | solution.py:630
  333.5 142.8 %all-reduce.7.cloned.1.call-start = ((), (), s32[]{:S(2)}) async-start(), calls=%async_computation.4 | async-start | bytes 2949120 | tf_op jit(solution)/shard_map/psum | solution.py:706
  346.0 41.4 %collective-permute-start.36 = (bf16[1,320,768]{2,1,0:T(8,128)(2,1)}, bf16[1,320,768]{2,1,0:T(8,128)(2,1)}, u32[]{:S(2)}, u32[]{:S(2)}) collective-permute-start(bf16[1,320,768]{2,1,0:T(8,128)(2,1)} %fusion.16), channel_id=1, source_target_pairs={{0,4},{4,0},{8,12},{12,8},{16,20},{20,16},{24,28},{28,24},{1,5},{5... | collective-permute-start | bytes 1474568 | tf_op jit(solution)/shard_map/ppermute | solution.py:630
  346.3 41.4 %collective-permute-start.37 = (bf16[1024,1280]{1,0:T(8,128)(2,1)}, bf16[1024,1280]{1,0:T(8,128)(2,1)}, u32[]{:S(2)}, u32[]{:S(2)}) collective-permute-start(bf16[1024,1280]{1,0:T(8,128)(2,1)} %output.2), channel_id=1, source_target_pairs={{0,1},{1,0},{2,3},{3,2},{4,5},{5,4},{6,7},{7,6},{8,9},{9,8},{10,11... | collective-permute-start | bytes 7864328 | tf_op jit(solution)/shard_map/ppermute | solution.py:630
  347.7 61.9 %collective-permute-start.38 = (bf16[1920,512]{1,0:T(8,128)(2,1)}, bf16[1920,512]{1,0:T(8,128)(2,1)}, u32[]{:S(2)}, u32[]{:S(2)}) collective-permute-start(bf16[1920,512]{1,0:T(8,128)(2,1)} %bitcast.278), channel_id=1, source_target_pairs={{0,2},{1,3},{2,0},{3,1},{4,6},{5,7},{6,4},{7,5},{8,10},{9,11},{10,... | collective-permute-start | bytes 5898248 | tf_op jit(solution)/shard_map/ppermute | solution.py:630
  392.3 143.1 %all-reduce.9.cloned.1.call-start = ((), (), s32[]{:S(2)}) async-start(), calls=%async_computation.5 | async-start | bytes 1966080 | tf_op jit(solution)/shard_map/psum | solution.py:706
  397.4 45.1 %collective-permute-start.46 = (bf16[1280,512]{1,0:T(8,128)(2,1)}, bf16[1280,512]{1,0:T(8,128)(2,1)}, u32[]{:S(2)}, u32[]{:S(2)}) collective-permute-start(bf16[1280,512]{1,0:T(8,128)(2,1)} %get-tuple-element.230.refs_1_.refs_6_), channel_id=1, source_target_pairs={{0,1},{1,0},{2,3},{3,2},{4,5},{5,4},{6,7},{7,6},{8,9},{9,8},{10,11... | collective-permute-start | bytes 3932168 | tf_op jit(solution)/shard_map/ppermute | solution.py:630
  397.5 45.0 %collective-permute-start.47 = (bf16[1280,512]{1,0:T(8,128)(2,1)}, bf16[1280,512]{1,0:T(8,128)(2,1)}, u32[]{:S(2)}, u32[]{:S(2)}) collective-permute-start(bf16[1280,512]{1,0:T(8,128)(2,1)} %get-tuple-element.229.refs_1_.refs_6_.refs_2_), channel_id=1, source_target_pairs={{0,1},{1,0},{2,3},{3,2},{4,5},{5,4},{6,7},{7,6},{8,9},{9,8},{10,11... | collective-permute-start | bytes 3932168 | tf_op jit(solution)/shard_map/ppermute | solution.py:630
  414.2 37.0 %collective-permute-start.44 = (bf16[3,320,512]{2,1,0:T(8,128)(2,1)S(1)}, bf16[3,320,512]{2,1,0:T(8,128)(2,1)}, u32[]{:S(2)}, u32[]{:S(2)}) collective-permute-start(bf16[3,320,512]{2,1,0:T(8,128)(2,1)S(1)} %fusion.8), channel_id=1, source_target_pairs={{0,4},{4,0},{8,12},{12,8},{16,20},{20,16},{24,28},{28,24},{1,5},{5... | collective-permute-start | bytes 2949128 | tf_op jit(solution)/shard_map/ppermute | solution.py:630
  441.6 53.2 %collective-permute-start.58 = (bf16[1280,1024]{1,0:T(8,128)(2,1)}, bf16[1280,1024]{1,0:T(8,128)(2,1)}, u32[]{:S(2)}, u32[]{:S(2)}) collective-permute-start(bf16[1280,1024]{1,0:T(8,128)(2,1)} %prepare.1.refs_1_), channel_id=1, source_target_pairs={{0,1},{1,0},{2,3},{3,2},{4,5},{5,4},{6,7},{7,6},{8,9},{9,8},{10,11... | collective-permute-start | bytes 7864328 | tf_op jit(solution)/shard_map/ppermute | solution.py:630
  485.8 134.9 %all-reduce.11.cloned.1.call-start = ((), (), s32[]{:S(2)}) async-start(), calls=%async_computation.6 | async-start | bytes 1310720 | tf_op jit(solution)/shard_map/psum | solution.py:706
  491.9 52.9 %collective-permute-start.63 = (bf16[3,320,768]{2,1,0:T(8,128)(2,1)}, bf16[3,320,768]{2,1,0:T(8,128)(2,1)}, u32[]{:S(2)}, u32[]{:S(2)}) collective-permute-start(bf16[3,320,768]{2,1,0:T(8,128)(2,1)} %all-reduce.7.cloned.1.call-done), channel_id=1, source_target_pairs={{0,4},{1,0},{2,6},{3,2},{4,5},{5,1},{6,7},{7,3},{8,12},{9,8},{10,1... | collective-permute-start | bytes 4423688 | tf_op jit(solution)/shard_map/ppermute | solution.py:719
  492.5 52.3 %collective-permute-start.64 = (bf16[3,320,768]{2,1,0:T(8,128)(2,1)}, bf16[3,320,768]{2,1,0:T(8,128)(2,1)}, u32[]{:S(2)}, u32[]{:S(2)}) collective-permute-start(bf16[3,320,768]{2,1,0:T(8,128)(2,1)} %all-reduce.7.cloned.1.call-done), channel_id=1, source_target_pairs={{1,4},{3,6},{4,1},{6,3},{9,12},{11,14},{12,9},{14,11},{17,20},{19,... | collective-permute-start | bytes 4423688 | tf_op jit(solution)/shard_map/ppermute | solution.py:719
  513.1 31.7 %collective-permute-start.61 = (bf16[640,960]{0,1:T(8,128)(2,1)}, bf16[640,960]{0,1:T(8,128)(2,1)}, u32[]{:S(2)}, u32[]{:S(2)}) collective-permute-start(bf16[640,960]{0,1:T(8,128)(2,1)} %copy.90), channel_id=1, source_target_pairs={{0,2},{1,3},{2,0},{3,1},{4,6},{5,7},{6,4},{7,5},{8,10},{9,11},{10,... | collective-permute-start | bytes 3686408 | tf_op jit(solution)/shard_map/ppermute | solution.py:630
  571.7 36.7 %collective-permute-start.67 = (bf16[1,320,640]{2,1,0:T(8,128)(2,1)S(1)}, bf16[1,320,640]{2,1,0:T(8,128)(2,1)S(1)}, u32[]{:S(2)}, u32[]{:S(2)}) collective-permute-start(bf16[1,320,640]{2,1,0:T(8,128)(2,1)S(1)} %add_convert_fusion.8), channel_id=1, source_target_pairs={{0,16},{4,20},{8,24},{12,28},{16,0},{20,4},{24,8},{28,12},{1,17},{... | collective-permute-start | bytes 1228808 | tf_op jit(solution)/shard_map/ppermute | solution.py:630
  (94 other events, 1036.0 us)
Sparse Core Ops, SparseCore 0:
  110.4 47.2 all-gather.3
  160.4 57.7 all-gather.5
  220.4 46.7 all-gather.7
  333.7 48.5 all-reduce.4
  392.4 64.2 all-reduce.6
  485.9 49.4 all-reduce.8
  570.7 49.9 all-reduce.10
